TPU v7x, 128 devices: a whole 4x4x4 slice. The times are simulated.
128 devices in a mesh: dp: 8 (over y_hi, z), fsdp: 16 (over y_lo, x, core).
Axes of the slice: x: 4, y: 4 (y_hi: 2, y_lo: 2; y = y_hi * 2 + y_lo), z: 4, core: 2. Of those that a mesh axis runs over, the one named last changes fastest.
Arguments:
- hidden: bfloat16 [32768, 8192], P(('dp', 'fsdp')), may hold values from -6 to 6
- inner_raw: bfloat16 [32768, 8192], P(('dp', 'fsdp')), may hold values from -6 to 6
- gate_raw: bfloat16 [32768, 8192], P(('dp', 'fsdp')), may hold values from -6 to 6
- step_raw: float32 [32768, 128], P(('dp', 'fsdp')), may hold values from -6 to 6
- proj_weight: bfloat16 [8192, 2048], P('fsdp'), may hold values from -0.0625 to 0.0625
- conv_weight: float32 [4, 10240], replicated, may hold values from -3 to 3
- conv_bias: float32 [10240], replicated, may hold values from -0.5 to 0.5
- decay_log: float32 [128], replicated, may hold values from -9 to -3.5
- step_bias: float32 [128], replicated, may hold values from -1 to 1
- norm_gain: float32 [8192], replicated, may hold values from 0.5 to 1.5
- ssm_state: bfloat16 [16, 128, 64, 256], P('dp', 'fsdp'), may hold values from -96 to 96
- conv_state: bfloat16 [16, 3, 10240], P('dp'), may hold values from -6 to 6
- slot_prompt: int32 [128], P(('dp', 'fsdp')), may hold values from 0 to 15, as said below
- slot_len: int32 [128], P(('dp', 'fsdp')), may hold values from 32 to 256, as said below
Outputs:
- mixed: bfloat16 [32768, 8192], P(('dp', 'fsdp'))
Inputs may be any that keep to these rules, and one draw needn't show every extreme that they name: `slot_prompt`: every prompt is continued by exactly 128 / 16 slots. `slot_len`: rows of a slot past its length are padding; some slot is full in every draw.
All inputs are finite; a program needn't handle non-finite values.
Results may differ from a plain program's by a relative error of at most 0.001.
Values may be sent and summed in bfloat16 or wider, within the bound.
A program may use at most 192 MiB of HBM per device.

v0:
```python
import jax
import jax.numpy as jnp
from jax import lax
from jax.sharding import PartitionSpec as P

BLK = 128


HIGHEST = lax.Precision.HIGHEST


def scan_blocks(inner_rows, b_rows, c_rows, step_sizes, decay_rate, start_state, block):
    row_count = inner_rows.shape[0]
    groups = start_state.shape[0]
    per_group = start_state.shape[1]
    head_dim = start_state.shape[2]
    state_dim = start_state.shape[3]
    features = groups * per_group * head_dim
    blocks = row_count // block
    log_rows = step_sizes * decay_rate[None, :]
    places = jnp.arange(block)
    causal = places[:, None] >= places[None, :]
    carry_state = start_state
    pieces_out = []
    for index in range(blocks):
        low = index * block
        inner_piece = inner_rows[low : low + block].reshape(block, groups, per_group, head_dim)
        b_piece = b_rows[low : low + block].reshape(block, groups, state_dim)
        c_piece = c_rows[low : low + block].reshape(block, groups, state_dim)
        step_piece = step_sizes[low : low + block].reshape(block, groups, per_group)
        log_piece = log_rows[low : low + block].reshape(block, groups, per_group)
        summed = jnp.cumsum(log_piece, axis=0)
        scores = jnp.einsum("tgn,sgn->gts", c_piece, b_piece, precision=HIGHEST)
        moved = jnp.transpose(summed, (1, 2, 0))
        spread_log = moved[:, :, :, None] - moved[:, :, None, :]
        weights = jnp.exp(jnp.where(causal[None, None], spread_log, -jnp.inf))
        mixing = weights * scores[:, None] * jnp.transpose(step_piece, (1, 2, 0))[:, :, None, :]
        within = jnp.einsum("gkts,sgkp->tgkp", mixing, inner_piece, precision=HIGHEST)
        carried = (
            jnp.einsum("tgn,gkpn->tgkp", c_piece, carry_state, precision=HIGHEST)
            * jnp.exp(summed)[:, :, :, None]
        )
        to_end = jnp.exp(summed[-1][None] - summed) * step_piece
        added_state = jnp.einsum(
            "sgk,sgkp,sgn->gkpn", to_end, inner_piece, b_piece, precision=HIGHEST
        )
        carry_state = jnp.exp(summed[-1])[:, :, None, None] * carry_state + added_state
        pieces_out.append((within + carried).reshape(block, features))
    return jnp.concatenate(pieces_out, axis=0)


def mixer(
    projected,
    inner_raw,
    gate_raw,
    step_raw,
    conv_weight,
    conv_bias,
    decay_log,
    step_bias,
    norm_gain,
    start_state,
    conv_rows,
    length,
    block,
):
    channels = jnp.concatenate([inner_raw.astype(jnp.float32), projected], axis=1)
    padded = jnp.concatenate([conv_rows.astype(jnp.float32), channels], axis=0)
    kernel_size = conv_weight.shape[0]
    row_count = channels.shape[0]
    convolved = jnp.zeros_like(channels) + conv_bias[None, :]
    for offset in range(kernel_size):
        convolved = convolved + conv_weight[offset][None, :] * padded[offset : offset + row_count]
    activated = jax.nn.silu(convolved)
    features = inner_raw.shape[1]
    state_cols = (channels.shape[1] - features) // 2
    heads = step_raw.shape[1]
    state_dim = start_state.shape[2]
    groups = state_cols // state_dim
    inner_rows = activated[:, :features]
    b_rows = activated[:, features : features + state_cols]
    c_rows = activated[:, features + state_cols :]
    step_sizes = jax.nn.softplus(step_raw + step_bias[None, :])
    decay_rate = -jnp.exp(decay_log)
    grouped_state = start_state.astype(jnp.float32).reshape(
        groups, heads // groups, start_state.shape[1], state_dim
    )
    output = scan_blocks(inner_rows, b_rows, c_rows, step_sizes, decay_rate, grouped_state, block)
    gated_out = output * jax.nn.silu(gate_raw.astype(jnp.float32))
    grouped = gated_out.reshape(row_count, groups, features // groups)
    scale_rows = lax.rsqrt(jnp.mean(grouped * grouped, axis=2, keepdims=True) + 1e-05)
    normed = (grouped * scale_rows).reshape(row_count, features) * norm_gain[None, :]
    live_rows = jnp.arange(row_count) < length
    return jnp.where(live_rows[:, None], normed, 0.0).astype(jnp.bfloat16)


def on_device(
    hidden,
    inner_raw,
    gate_raw,
    step_raw,
    proj_weight,
    conv_weight,
    conv_bias,
    decay_log,
    step_bias,
    norm_gain,
    ssm_state,
    conv_state,
    slot_prompt,
    slot_len,
):
    prompt = slot_prompt[0]
    length = slot_len[0]
    projected = jnp.dot(
        hidden,
        lax.all_gather(proj_weight, "fsdp", axis=0, tiled=True),
        preferred_element_type=jnp.float32,
    )
    states = lax.all_gather(ssm_state, "dp", axis=0, tiled=True)
    conv_all = lax.all_gather(conv_state, "dp", axis=0, tiled=True)
    conv_rows = lax.dynamic_index_in_dim(conv_all, prompt, 0, keepdims=False)
    owners = lax.all_gather(slot_prompt, "fsdp", axis=0, tiled=True)
    picker = (jnp.arange(states.shape[0])[None, :] == owners[:, None]).astype(jnp.bfloat16)
    outgoing = jnp.einsum(
        "gq,qhpn->ghpn", picker, states, preferred_element_type=jnp.float32
    ).astype(jnp.bfloat16)
    arrived = lax.all_to_all(outgoing, "fsdp", split_axis=0, concat_axis=0, tiled=True)
    all_heads = arrived.reshape(
        arrived.shape[0] * arrived.shape[1], arrived.shape[2], arrived.shape[3]
    )
    start_state, conv_rows = (all_heads, conv_rows)
    return mixer(
        projected,
        inner_raw,
        gate_raw,
        step_raw,
        conv_weight,
        conv_bias,
        decay_log,
        step_bias,
        norm_gain,
        start_state,
        conv_rows,
        length,
        BLK,
    )


def solution(mesh):
    in_specs = (
        P(("dp", "fsdp"), None),
        P(("dp", "fsdp"), None),
        P(("dp", "fsdp"), None),
        P(("dp", "fsdp"), None),
        P("fsdp", None),
        P(),
        P(),
        P(),
        P(),
        P(),
        P("dp", "fsdp", None, None),
        P("dp", None, None),
        P(("dp", "fsdp")),
        P(("dp", "fsdp")),
    )
    out_specs = P(("dp", "fsdp"), None)
    return jax.shard_map(
        on_device, mesh=mesh, in_specs=in_specs, out_specs=out_specs, check_vma=False
    )
```

profile of v0, /device:TPU:1, one launch (start us, length us, event | category | flops | bytes accessed | tf_op | source)
XLA Modules:
  0.0 501.2 jit_solution(10827778376596140717)
XLA Ops:
  6.5 0.7 all-gather.5.cloned.1.call-update
  8.0 6.4 %copy.126 = bf16[256,8192]{0,1:T(8,128)(2,1)} copy(bf16[256,8192]{1,0:T(8,128)(2,1)} %param.15) | data formatting | bytes 8388608 | tf_op args[1]
  14.4 6.1 %convert_element_type.25 = f32[256,8192]{0,1:T(8,128)} convert(bf16[256,8192]{0,1:T(8,128)(2,1)} %copy.126) | non-fusion elementwise | flops 2097152 | bytes 12582912 | tf_op jit(solution)/shard_map/convert_element_type | solution.py:67
  21.3 35.5 %all_gather.12 = bf16[16,3,10240]{2,1,0:T(4,128)(2,1)S(1)} all-gather(bf16[2,3,10240]{2,1,0:T(4,128)(2,1)S(1)} %copy.125), channel_id=1, replica_groups=mesh['dp'=8,'fsdp'=16] {'dp'}, dimensions={0}, use_global_device_ids=true | all-gather | bytes 1105920 | tf_op jit(solution)/shard_map/all_gather | solution.py:121
  56.9 3.2 copy.128
  63.8 16.2 %all-reduce = s32[16]{0:T(128)S(1)} all-reduce(s32[16]{0:T(128)S(1)} %dynamic-update-slice), channel_id=1, replica_groups=mesh['dp'=8,'fsdp'=16] {'fsdp'}, use_global_device_ids=true, to_apply=%add | all-reduce | flops 16 | bytes 128
  80.1 9.5 %all-gather.5.cloned.1.call-done = bf16[16,8,64,256]{3,2,1,0:T(8,128)(2,1)} async-done(((bf16[2,8,64,256]{3,2,1,0:T(8,128)(2,1)}), bf16[16,8,64,256]{3,2,1,0:T(8,128)(2,1)}) %all-gather.5.cloned.1.call-update) | async-done | bytes 4194320 | tf_op jit(solution)/shard_map/all_gather | solution.py:120
  89.7 4.7 fusion.46
  94.4 3.6 copy.136
  98.0 5.8 %all-to-all-start = ((bf16[16,8,64,256]{3,2,1,0:T(8,128)(2,1)}), bf16[16,8,64,256]{3,2,1,0:T(8,128)(2,1)}, u32[]{:S(2)}, u32[]{:S(2)}) async-start(bf16[16,8,64,256]{3,2,1,0:T(8,128)(2,1)} %copy.136), calls=%async_computation | async-start | bytes 8388608 | tf_op jit(solution)/shard_map/all_to_all | solution.py:128
  103.8 202.5 %all-gather.3.cloned.1.call-done = bf16[8192,2048]{1,0:T(8,128)(2,1)} async-done(((bf16[512,2048]{1,0:T(8,128)(2,1)}), bf16[8192,2048]{1,0:T(8,128)(2,1)}) %all-gather.3.cloned.1.call-update) | async-done | bytes 33554448 | tf_op jit(solution)/shard_map/all_gather | solution.py:117
  306.4 18.1 %fusion.69 = f32[256,2048]{0,1:T(8,128)S(1)} fusion(bf16[256,8192]{1,0:T(8,128)(2,1)} %param.14, bf16[8192,2048]{1,0:T(8,128)(2,1)} %all-gather.3.cloned.1.call-done), kind=kOutput, calls=%fused_computation.83 | convolution fusion | flops 8589934592 | bytes 39845888 | tf_op jit(solution)/shard_map/dot_general | solution.py:115
  324.5 15.2 %maximum_maximum_fusion = f32[259,10240]{0,1:T(8,128)} fusion(f32[256,2048]{0,1:T(8,128)S(1)} %fusion.69, f32[256,8192]{0,1:T(8,128)} %convert_element_type.25, f32[3,10240]{0,1:T(8,128)} %copy.128), kind=kLoop, calls=%fused_computation | loop fusion | flops 5304320 | bytes 21217280 | tf_op jit(solution)/shard_map/concatenate | solution.py:68
  339.7 23.5 %divide_multiply_fusion = f32[256,10240]{0,1:T(8,128)} fusion(f32[256,2048]{0,1:T(8,128)S(1)} %fusion.69, f32[256,8192]{0,1:T(8,128)} %convert_element_type.25, f32[259,10240]{0,1:T(8,128)} %maximum_maximum_fusion, f32[10240]{0:T(1024)S(1)} %bitcast.124, f32[10240]{0:T(1024)S(1)} %bitcast.125, f32[10240]{0:T(1024)S(1)} %bitcast.123, f32[10240]{0:T(1024)S(1)} %bitcast.122, ...), kind=kLoop, calls=%fused_computation.11 | loop fusion | flops 34078720 | bytes 52633600 | tf_op jit(solution)/shard_map/jit(silu)/mul | solution.py:74
  363.1 1.7 fusion.61
  364.8 1.0 fusion.71
  365.9 6.0 %fusion.62 = (f32[128,8192]{0,1:T(8,128)}, f32[128,8192]{0,1:T(8,128)S(1)}) fusion(f32[256,10240]{0,1:T(8,128)} %divide_multiply_fusion), kind=kLoop, calls=%fused_computation.76 | loop fusion | bytes 16777216 | tf_op jit(solution)/shard_map/slice | solution.py:27
  371.9 2.0 copy-done.2
  373.8 9.1 %fusion.31 = f32[4,32,64,256]{3,2,1,0:T(8,128)} fusion(f32[128,4,256,1]{0,2,3,1:T(8,128)S(1)} %bitcast.103, f32[128,4,32,64]{0,3,2,1:T(8,128)S(1)} %bitcast.100, f32[128,4,32]{0,2,1:T(8,128)S(1)} %copy.145), kind=kOutput, calls=%fused_computation.42 | convolution fusion | flops 3222274048 | bytes 13172736 | tf_op jit(solution)/shard_map/sgk,sgkp,sgn->gkpn/dot_general | solution.py:44
  383.0 11.4 %fusion.8 = f32[4,32,64,128]{3,2,1,0:T(8,128)S(1)} fusion(f32[128,4,256,1]{0,2,3,1:T(8,128)S(1)} %bitcast.106, f32[4,32,64,256]{3,2,1,0:T(8,128)} %fusion.31, f32[4,32]{1,0:T(4,128)S(1)} %fusion.59, bf16[4,32,64,256]{3,2,1,0:T(8,128)(2,1)} %bitcast.86), kind=kOutput, calls=%fused_computation.17 | convolution fusion | flops 3227516928 | bytes 17302016 | tf_op jit(solution)/shard_map/tgn,gkpn->tgkp/dot_general | solution.py:40
  394.4 18.5 %fusion.24 = f32[128,4,32,64]{0,3,2,1:T(8,128)} fusion(f32[4,32,64,128]{3,2,1,0:T(8,128)S(1)} %fusion.8, f32[128,4,32]{0,2,1:T(8,128)S(1)} %copy.148, f32[128,4,32,64]{0,3,2,1:T(8,128)S(1)} %bitcast.110, f32[4,32,128]{2,1,0:T(8,128)S(1)} %bitcast.126, f32[4,128,128]{2,1,0:T(8,128)S(1)} %fusion.71, f32[4,32,128]{2,1,0:T(8,128)S(1)} %copy.140, ...), kind=kOutput, calls=%fused_computation.34 | convolution fusion | flops 1621098496 | bytes 13058048 | tf_op jit(solution)/shard_map/gkts,sgkp->tgkp/dot_general | solution.py:38
  412.9 5.6 %copy.150 = f32[128,8192]{1,0:T(8,128)} copy(f32[128,8192]{0,1:T(8,128)} %bitcast.109) | data formatting | bytes 8388608 | tf_op jit(solution)/shard_map/reshape | solution.py:48
  418.6 1.0 fusion.70
  419.6 18.5 %fusion.18 = f32[4,32,64,128]{3,2,1,0:T(8,128)S(1)} fusion(f32[128,4,32,64]{0,3,2,1:T(8,128)} %bitcast.101, f32[4,32,128]{2,1,0:T(8,128)S(1)} %bitcast.119, f32[4,128,128]{2,1,0:T(8,128)S(1)} %fusion.70, f32[4,32,128]{2,1,0:T(8,128)S(1)} %copy.131, pred[128,128]{1,0:T(8,128)(4,1)S(1)} %iota_compare_fusion), kind=kOutput, calls=%fused_computation.27 | convolution fusion | flops 1619001344 | bytes 8798208 | tf_op jit(solution)/shard_map/gkts,sgkp->tgkp/dot_general | solution.py:38
  438.1 7.8 %fusion.25 = f32[128,4,32,64]{0,3,2,1:T(8,128)} fusion(f32[4,32,64,128]{3,2,1,0:T(8,128)S(1)} %fusion.18, f32[128,4,256,1]{0,2,3,1:T(8,128)S(1)} %bitcast.108, f32[128,4,32]{0,2,1:T(8,128)S(1)} %copy.138, bf16[4,32,64,256]{3,2,1,0:T(8,128)(2,1)} %bitcast.88), kind=kOutput, calls=%fused_computation.36 | convolution fusion | flops 3223322624 | bytes 13172736 | tf_op jit(solution)/shard_map/tgn,gkpn->tgkp/dot_general | solution.py:40
  445.9 5.6 %copy.149 = f32[128,8192]{1,0:T(8,128)} copy(f32[128,8192]{0,1:T(8,128)} %bitcast.102) | data formatting | bytes 8388608 | tf_op jit(solution)/shard_map/reshape | solution.py:48
  451.5 7.8 %fusion.60 = f32[256,8192]{1,0:T(8,128)} fusion(bf16[256,8192]{1,0:T(8,128)(2,1)} %param.16, f32[128,8192]{1,0:T(8,128)} %copy.150, f32[128,8192]{1,0:T(8,128)} %copy.149), kind=kLoop, calls=%fused_computation.74 | loop fusion | flops 16777216 | bytes 20971520 | tf_op jit(solution)/shard_map/mul | solution.py:91
  459.3 10.8 %mul.176 = f32[256,4,2048]{2,1,0:T(4,128)} reshape(f32[256,8192]{1,0:T(8,128)} %fusion.60) | data formatting | bytes 16777216 | tf_op jit(solution)/shard_map/mul | solution.py:91
  470.1 4.5 reduce_sum.9
  474.7 1.1 mul.177
  475.9 11.0 %copy.168 = f32[32,8,4,2048]{3,1,2,0:T(8,128)} copy(f32[32,8,4,2048]{3,2,1,0:T(4,128)S(1)} %bitcast.98) | data formatting | bytes 16777216
  486.9 7.2 %select_convert_fusion = bf16[256,8192]{1,0:T(8,128)(2,1)} fusion(f32[256,8192]{1,0:T(8,128)} %bitcast.99, f32[8192]{0:T(1024)S(1)} %copy-done.9, pred[256]{0:T(512)(128)(4,1)S(1)} %iota_compare_fusion.2, bf16[256,8192]{1,0:T(8,128)(2,1)S(1)} %copy-done.3, f32[128,8192]{1,0:T(8,128)S(1)} %copy-done, f32[128,8192]{1,0:T(8,128)S(1)} %copy-done.1), kind=kLoop, calls=%fused_computation.16 | loop fusion | flops 23068672 | bytes 25198848 | tf_op jit(solution)/shard_map/convert_element_type | solution.py:94
  (57 shorter events, 4.0 us)
Async XLA Ops:
  6.5 83.1 %all-gather.5.cloned.1.call-start = ((), (), s32[]{:S(2)}) async-start(), calls=%async_computation.2 | async-start | bytes 4718592 | tf_op jit(solution)/shard_map/all_gather | solution.py:120
  7.3 299.1 %all-gather.3.cloned.1.call-start = ((), (), s32[]{:S(2)}) async-start(), calls=%async_computation.1 | async-start | bytes 35651584 | tf_op jit(solution)/shard_map/all_gather | solution.py:117
  8.0 12.5 %copy-start.7 = (bf16[2,3,10240]{2,0,1:T(2,128)(2,1)S(1)}, bf16[2,3,10240]{2,0,1:T(2,128)(2,1)}, u32[]{:S(2)}) copy-start(bf16[2,3,10240]{2,0,1:T(2,128)(2,1)} %param.25) | copy-start | bytes 368644
  14.4 45.7 %copy-start.6 = (f32[256,128]{1,0:T(8,128)S(1)}, f32[256,128]{1,0:T(8,128)}, u32[]{:S(2)}) copy-start(f32[256,128]{1,0:T(8,128)} %param.17) | copy-start | bytes 393220
  14.4 45.8 %copy-start.11 = (f32[128]{0:T(128)S(1)}, f32[128]{0:T(128)}, u32[]{:S(2)}) copy-start(f32[128]{0:T(128)} %param.21) | copy-start | bytes 1540
  14.4 45.8 %copy-start.10 = (f32[128]{0:T(128)S(1)}, f32[128]{0:T(128)}, u32[]{:S(2)}) copy-start(f32[128]{0:T(128)} %param.22) | copy-start | bytes 1540
  20.5 42.1 %copy-start.12 = (u32[128]{0:T(128)S(1)}, u32[128]{0:T(128)}, u32[]{:S(2)}) copy-start(u32[128]{0:T(128)} %constant.32) | copy-start | bytes 1540
  20.5 59.5 %copy-start.5 = (f32[4,10240]{1,0:T(4,128)S(1)}, f32[4,10240]{1,0:T(4,128)}, u32[]{:S(2)}) copy-start(f32[4,10240]{1,0:T(4,128)} %param.19) | copy-start | bytes 491524
  98.0 285.0 %all-to-all-start = ((bf16[16,8,64,256]{3,2,1,0:T(8,128)(2,1)}), bf16[16,8,64,256]{3,2,1,0:T(8,128)(2,1)}, u32[]{:S(2)}, u32[]{:S(2)}) async-start(bf16[16,8,64,256]{3,2,1,0:T(8,128)(2,1)} %copy.136), calls=%async_computation | async-start | bytes 8388608 | tf_op jit(solution)/shard_map/all_to_all | solution.py:128
  324.5 15.2 %copy-start.8 = (f32[10240]{0:T(1024)S(1)}, f32[10240]{0:T(1024)}, u32[]{:S(2)}) copy-start(f32[10240]{0:T(1024)} %param.20) | copy-start | bytes 122884
  371.9 2.0 copy-start.2
  383.0 11.4 %copy-start.4 = (f32[128,8192]{0,1:T(8,128)S(1)}, f32[128,8192]{0,1:T(8,128)}, u32[]{:S(2)}) copy-start(f32[128,8192]{0,1:T(8,128)} %get-tuple-element.11) | copy-start | bytes 12582916
  475.8 11.1 %copy-start = (f32[128,8192]{1,0:T(8,128)S(1)}, f32[128,8192]{1,0:T(8,128)}, u32[]{:S(2)}) copy-start(f32[128,8192]{1,0:T(8,128)} %copy.150) | copy-start | bytes 12582916
  475.9 11.1 %copy-start.1 = (f32[128,8192]{1,0:T(8,128)S(1)}, f32[128,8192]{1,0:T(8,128)}, u32[]{:S(2)}) copy-start(f32[128,8192]{1,0:T(8,128)} %copy.149) | copy-start | bytes 12582916
  475.9 11.1 %copy-start.3 = (bf16[256,8192]{1,0:T(8,128)(2,1)S(1)}, bf16[256,8192]{1,0:T(8,128)(2,1)}, u32[]{:S(2)}) copy-start(bf16[256,8192]{1,0:T(8,128)(2,1)} %param.16) | copy-start | bytes 12582916
  475.9 11.1 %copy-start.9 = (f32[8192]{0:T(1024)S(1)}, f32[8192]{0:T(1024)}, u32[]{:S(2)}) copy-start(f32[8192]{0:T(1024)} %param.23) | copy-start | bytes 98308
Sparse Core Ops, SparseCore 0:
  9.7 79.9 all-gather.4
  91.4 214.9 all-gather.2
where the time goes:
time: 508 us; the launch traced here: 501 us
  waiting for transfers between devices  213 us (42%)
  matrix products  90.3 us (18%)
  other arithmetic  64.8 us (13%)
  local copies, waits for them, and re-layouts  59.8 us (12%)
  blocking collectives  51.7 us (10%)
  between operations  15.2 us (3%)
  starting transfers between devices  5.89 us (1%)
    all_gather x1, waiting for transfers between devices, on_device(): lax.all_gather(proj_weight, 'fsdp', axis=0, tiled=True)  203 us
    dot_general x2, matrix products, scan_blocks(): jnp.einsum('gkts,sgkp->tgkp', mixing, inner_piece, precision=HIGHEST)  37.1 us
    all_gather x1, blocking collectives, on_device(): conv_all = lax.all_gather(conv_state, 'dp', axis=0, tiled=True)  35.5 us
    mul x1, other arithmetic, mixer(): activated = jax.nn.silu(convolved)  23.5 us
    unnamed x34, local copies, waits for them, and re-layouts  20.9 us
    dot_general x2, matrix products, scan_blocks(): jnp.einsum('tgn,gkpn->tgkp', c_piece, carry_state, precision=HIGHEST)  19.2 us
    dot_general x1, matrix products, on_device(): jnp.dot(hidden, lax.all_gather(proj_weight, 'fsdp', axis=0, tiled=True),...  18.1 us
    unnamed x1, blocking collectives  16.2 us
  transfers between devices with their start and end apart: 3, of which 2 were waited for; matrix products, arithmetic and copies ran while one was open for 20% of the time, Pallas kernels for 0%

commit v1 on v0

v1 whole, which is shorter than its diff:
```python
import jax
import jax.numpy as jnp
from jax import lax
from jax.experimental import pallas as pl
from jax.experimental.pallas import tpu as pltpu
from jax.sharding import PartitionSpec as P

F32 = jnp.float32
BF16 = jnp.bfloat16
PIECE = 512


def split_two(value):
    high = value.astype(BF16)
    return high, (value - high.astype(F32)).astype(BF16)


def dot_nn(left, right):
    return jnp.dot(left, right, preferred_element_type=F32)


def dot_nt(left, right):
    return lax.dot_general(left, right, (((1,), (1,)), ((), ())), preferred_element_type=F32)


def silu(value):
    half = 0.5 * value
    return half + half * jnp.tanh(half)


def convolve(pad_ref, rows, first, taps, bias):
    count = rows.shape[0]
    pad_ref[5:8, :] = first
    pad_ref[8 : 8 + count, :] = rows
    total = taps[3:4, :] * rows + bias
    for k in range(3):
        total = total + taps[k : k + 1, :] * pad_ref[5 + k : 5 + k + count, :]
    return total


def before_kernel(
    inner_ref, gate_ref, step_ref, decay_ref, step_bias_ref, taps_ref, bias_ref, first_ref,
    high_ref, low_ref, gate_out_ref,
    pad_ref, heads_ref, grow_ref, fall_ref,
):
    tile = pl.program_id(0)
    count = inner_ref.shape[0]
    width = inner_ref.shape[1]
    heads = step_ref.shape[1]

    @pl.when(tile == 0)
    def _():
        raw = step_ref[...] + step_bias_ref[...]
        steps = jnp.maximum(raw, 0.0) + jnp.log1p(jnp.exp(-jnp.abs(raw)))
        logs = -jnp.exp(decay_ref[...]) * steps
        place = lax.broadcasted_iota(jnp.int32, (count, count), 0)
        other = lax.broadcasted_iota(jnp.int32, (count, count), 1)
        lower = jnp.where(place >= other, 1.0, 0.0).astype(BF16)
        top = logs.astype(BF16)
        rest = logs - top.astype(F32)
        mid, last = split_two(rest)
        summed = dot_nn(lower, top) + (dot_nn(lower, mid) + dot_nn(lower, last))
        grow_ref[:, :heads], grow_ref[:, heads:] = split_two(steps * jnp.exp(-summed))
        fall_ref[:, :heads], fall_ref[:, heads:] = split_two(jnp.exp(summed))
        head = lax.broadcasted_iota(jnp.int32, (2 * heads, width), 0)
        column = lax.broadcasted_iota(jnp.int32, (2 * heads, width), 1)
        heads_ref[...] = jnp.where(head >= heads, head - heads, head) - column // 64

    spread = jnp.where(heads_ref[...] == tile * (width // 64), 1.0, 0.0).astype(BF16)
    rows = inner_ref[...].astype(F32)
    active = silu(convolve(pad_ref, rows, first_ref[...].astype(F32), taps_ref[...], bias_ref[...]))
    high_ref[...], low_ref[...] = split_two(active * dot_nn(grow_ref[...], spread))
    gate_out_ref[...] = silu(gate_ref[...].astype(F32)) * dot_nn(fall_ref[...], spread)


def before(inner_raw, gate_raw, step_raw, decay_log, step_bias, conv_weight, conv_bias, conv_rows):
    count, features = inner_raw.shape
    heads = step_raw.shape[1]
    width = PIECE
    across = lambda rows: pl.BlockSpec((rows, width), lambda j: (0, j))
    whole = lambda rows: pl.BlockSpec((rows, heads), lambda j: (0, 0))
    return pl.pallas_call(
        before_kernel,
        grid=(features // width,),
        in_specs=[
            across(count), across(count), whole(count), whole(1), whole(1),
            across(4), across(1), across(3),
        ],
        out_specs=[across(count), across(count), across(count)],
        out_shape=[
            jax.ShapeDtypeStruct((count, features), BF16),
            jax.ShapeDtypeStruct((count, features), BF16),
            jax.ShapeDtypeStruct((count, features), F32),
        ],
        scratch_shapes=[
            pltpu.VMEM((count + 8, width), F32),
            pltpu.VMEM((2 * heads, width), jnp.int32),
            pltpu.VMEM((count, 2 * heads), BF16),
            pltpu.VMEM((count, 2 * heads), BF16),
        ],
        compiler_params=pltpu.CompilerParams(vmem_limit_bytes=32 * 2**20),
        name="before_scan",
    )(inner_raw, gate_raw, step_raw, decay_log, step_bias, conv_weight, conv_bias, conv_rows)


def after_kernel(
    length_ref, b_ref, c_ref, b_taps_ref, c_taps_ref, b_bias_ref, c_bias_ref, b_first_ref, c_first_ref,
    state_ref, high_ref, low_ref, gate_ref, gain_ref, out_ref, pad_ref, gated_ref,
):
    count = b_ref.shape[0]
    features = high_ref.shape[1]

    def channel(rows, first, taps, bias):
        return split_two(
            silu(convolve(pad_ref, rows[...], first[...].astype(F32), taps[...], bias[...]))
        )

    b_high, b_low = channel(b_ref, b_first_ref, b_taps_ref, b_bias_ref)
    c_high, c_low = channel(c_ref, c_first_ref, c_taps_ref, c_bias_ref)
    scores = dot_nt(c_high, b_high) + (dot_nt(c_high, b_low) + dot_nt(c_low, b_high))
    place = lax.broadcasted_iota(jnp.int32, (count, count), 0)
    other = lax.broadcasted_iota(jnp.int32, (count, count), 1)
    m_high, m_low = split_two(jnp.where(place >= other, scores, 0.0))
    squares = jnp.zeros((count, 128), F32)
    for low in range(0, features, PIECE):
        cols = slice(low, low + PIECE)
        state = state_ref[cols, :]
        total = dot_nt(c_high, state) + dot_nt(c_low, state)
        total = total + dot_nn(m_high, high_ref[:, cols])
        total = total + (dot_nn(m_high, low_ref[:, cols]) + dot_nn(m_low, high_ref[:, cols]))
        gated = total * gate_ref[:, cols]
        gated_ref[:, cols] = gated
        for at in range(0, PIECE, 128):
            part = gated[:, at : at + 128]
            squares = squares + part * part
    mean = jnp.sum(squares, axis=1, keepdims=True) * (1.0 / features)
    row = lax.broadcasted_iota(jnp.int32, (count, 1), 0)
    scale = jnp.where(row < length_ref[0], lax.rsqrt(mean + 1e-05), 0.0)
    for low in range(0, features, PIECE):
        cols = slice(low, low + PIECE)
        out_ref[:, cols] = (gated_ref[:, cols] * scale * gain_ref[:, cols]).astype(BF16)


def after(length, projected, conv_weight, conv_bias, conv_rows, state, high, low, gate, norm_gain):
    count, features = high.shape
    n = state.shape[1]
    groups = projected.shape[1] // (2 * n)
    width = features // groups
    first_b = features // n
    at = lambda rows, base: pl.BlockSpec((rows, n), lambda g, base=base: (0, base + g))
    wide = lambda rows: pl.BlockSpec((rows, width), lambda g: (0, g))
    return pl.pallas_call(
        after_kernel,
        grid=(groups,),
        in_specs=[
            pl.BlockSpec(memory_space=pltpu.SMEM),
            at(count, 0), at(count, groups),
            at(4, first_b), at(4, first_b + groups),
            at(1, first_b), at(1, first_b + groups),
            at(3, first_b), at(3, first_b + groups),
            pl.BlockSpec((width, n), lambda g: (g, 0)),
            wide(count), wide(count), wide(count), wide(1),
        ],
        out_specs=wide(count),
        out_shape=jax.ShapeDtypeStruct((count, features), BF16),
        scratch_shapes=[pltpu.VMEM((count + 8, n), F32), pltpu.VMEM((count, width), F32)],
        compiler_params=pltpu.CompilerParams(vmem_limit_bytes=40 * 2**20),
        name="scan_and_norm",
    )(
        length, projected, projected, conv_weight, conv_weight, conv_bias, conv_bias,
        conv_rows, conv_rows, state, high, low, gate, norm_gain,
    )


def on_device(
    hidden, inner_raw, gate_raw, step_raw, proj_weight, conv_weight, conv_bias, decay_log, step_bias,
    norm_gain, ssm_state, conv_state, slot_prompt, slot_len,
):
    prompt = slot_prompt[0]
    conv_bias = conv_bias[None, :]
    conv_all = lax.all_gather(conv_state, "dp", axis=0, tiled=True)
    conv_rows = lax.dynamic_index_in_dim(conv_all, prompt, 0, keepdims=False)
    states = lax.all_gather(ssm_state, "dp", axis=0, tiled=True)
    owners = lax.all_gather(slot_prompt, "fsdp", axis=0, tiled=True)
    high, low, gate = before(
        inner_raw, gate_raw, step_raw, decay_log[None, :], step_bias[None, :],
        conv_weight, conv_bias, conv_rows,
    )
    projected = jnp.dot(
        hidden,
        lax.all_gather(proj_weight, "fsdp", axis=0, tiled=True),
        preferred_element_type=F32,
    )
    outgoing = jnp.take(states, owners, axis=0)
    arrived = lax.all_to_all(outgoing, "fsdp", split_axis=0, concat_axis=0, tiled=True)
    state = arrived.reshape(-1, arrived.shape[3])
    return after(
        slot_len, projected, conv_weight, conv_bias, conv_rows, state, high, low, gate,
        norm_gain[None, :],
    )


def solution(mesh):
    rows = P(("dp", "fsdp"), None)
    in_specs = (
        rows, rows, rows, rows, P("fsdp", None), P(), P(), P(), P(), P(),
        P("dp", "fsdp", None, None), P("dp", None, None), P(("dp", "fsdp")), P(("dp", "fsdp")),
    )
    return jax.shard_map(on_device, mesh=mesh, in_specs=in_specs, out_specs=rows, check_vma=False)
```

time: 508 us -> 351 us (0.69); the launches traced: 501 us -> 350 us
  matrix products: 90.3 us -> 16.2 us
  other arithmetic: 64.8 us -> 4.69 us
  waiting for transfers between devices: 213 us -> 165 us
  blocking collectives: 51.7 us -> 97.9 us
  local copies, waits for them, and re-layouts: 59.8 us -> 18.6 us
  Pallas kernels: 0 us -> 26.8 us
    all_gather x1, waiting for transfers between devices: 203 us -> 102 us  [on_device(): lax.all_gather(proj_weight, 'fsdp', axis=0, tiled=True)]
    dot_general x8 -> x0, matrix products: 72.2 us -> none  [the longest x2 37.1 us: scan_blocks(): jnp.einsum('gkts,sgkp->tgkp', mixing, inner_piece, precision=HIGHEST)]
    all_gather x1, waiting for transfers between devices: 9.53 us -> 61.6 us  [on_device(): states = lax.all_gather(ssm_state, 'dp', axis=0, tiled=True)]
    all_gather x1, blocking collectives: 35.5 us -> 87.1 us  [on_device(): conv_all = lax.all_gather(conv_state, 'dp', axis=0, tiled=True)]
    mul x3 -> x0, other arithmetic: 31.4 us -> none  [the longest x1 23.5 us: mixer(): activated = jax.nn.silu(convolved)]
    pallas_call x0 -> x2, Pallas kernels: none -> 26.8 us  [the longest x1 14 us: before(): pl.pallas_call(before_kernel, grid=(features // width,), in_specs=[across...]
    concatenate x1 -> x0, other arithmetic: 15.2 us -> none  [mixer(): padded = jnp.concatenate([conv_rows.astype(jnp.float32), channels], axis=0)]
    convert_element_type x3 -> x0, other arithmetic: 13.3 us -> none  [the longest x1 7.18 us: mixer(): return jnp.where(live_rows[:, None], normed, 0.0).astype(jnp.bfloat16)]
  transfers between devices with their start and end apart: 3 -> 3, of which waited for: 2 -> 2; matrix products, arithmetic and copies ran while one was open for 20% -> 8% of each run, Pallas kernels for 0% -> 4%
where the time goes in v1:
time: 351 us; the launch traced here: 350 us
  waiting for transfers between devices  165 us (47%)
  blocking collectives  97.9 us (28%)
  Pallas kernels  26.8 us (8%)
  local copies, waits for them, and re-layouts  18.6 us (5%)
  matrix products  16.2 us (5%)
  between operations  14.8 us (4%)
  starting transfers between devices  6.1 us (2%)
  other arithmetic  4.69 us (1%)
    all_gather x1, waiting for transfers between devices, on_device(): lax.all_gather(proj_weight, 'fsdp', axis=0, tiled=True)  102 us
    all_gather x1, blocking collectives, on_device(): conv_all = lax.all_gather(conv_state, 'dp', axis=0, tiled=True)  87.1 us
    all_gather x1, waiting for transfers between devices, on_device(): states = lax.all_gather(ssm_state, 'dp', axis=0, tiled=True)  61.6 us
    dot_general x1, matrix products, on_device(): jnp.dot(hidden, lax.all_gather(proj_weight, 'fsdp', axis=0, tiled=True),...  16.2 us
    pallas_call x1, Pallas kernels, before(): pl.pallas_call(before_kernel, grid=(features // width,), in_specs=[across...  14 us
    unnamed x26, local copies, waits for them, and re-layouts  13.6 us
    pallas_call x1, Pallas kernels, after(): pl.pallas_call(after_kernel, grid=(groups,), in_specs=[pl.BlockSpec(memor...  12.8 us
    unnamed x1, blocking collectives  10.8 us
  transfers between devices with their start and end apart: 3, of which 2 were waited for; matrix products, arithmetic and copies ran while one was open for 8% of the time, Pallas kernels for 4%

profile of v1, /device:TPU:1, one launch (start us, length us, event | category | flops | bytes accessed | tf_op | source)
XLA Modules:
  0.0 350.3 jit_solution(13211325312977855190)
XLA Ops:
  6.5 0.0 all-gather.5.cloned.1.call-start
  6.5 0.7 all-gather.5.cloned.1.call-update
  7.3 0.0 all-gather.3.cloned.1.call-start
  7.3 0.7 all-gather.3.cloned.1.call-update
  8.0 1.0 copy.15
  9.7 1.2 dynamic-slice
  10.9 0.8 dynamic-update-slice
  11.7 10.8 %all-reduce = s32[16]{0:T(128)S(1)} all-reduce(s32[16]{0:T(128)S(1)} %dynamic-update-slice), channel_id=1, replica_groups=mesh['dp'=8,'fsdp'=16] {'fsdp'}, use_global_device_ids=true, to_apply=%add | all-reduce | flops 16 | bytes 128
  22.5 61.6 %all-gather.5.cloned.1.call-done = bf16[16,8,64,256]{3,2,1,0:T(8,128)(2,1)} async-done(((bf16[2,8,64,256]{3,2,1,0:T(8,128)(2,1)}), bf16[16,8,64,256]{3,2,1,0:T(8,128)(2,1)}) %all-gather.5.cloned.1.call-update) | async-done | bytes 4194320 | tf_op jit(solution)/shard_map/all_gather | solution.py:183
  84.1 5.0 %gather_fusion = bf16[16,8,64,256]{3,2,1,0:T(8,128)(2,1)} fusion(bf16[16,8,64,256]{3,2,1,0:T(8,128)(2,1)} %all-gather.5.cloned.1.call-done, s32[1024]{0:T(1024)S(1)} %pad_clamp_fusion), kind=kCustom, calls=%fused_computation | custom fusion | bytes 8388672 | tf_op jit(solution)/shard_map/jit(_take)/gather | solution.py:194
  89.2 4.7 %broadcast_select_fusion = bf16[16,8,64,256]{3,2,1,0:T(8,128)(2,1)} fusion(bf16[16,8,64,256]{3,2,1,0:T(8,128)(2,1)} %gather_fusion, pred[16]{0:T(512)(128)(4,1)S(1)} %compare_and_fusion), kind=kLoop, calls=%fused_computation.1 | loop fusion | flops 2097152 | bytes 8388624 | tf_op jit(solution)/shard_map/jit(_take)/select_n | solution.py:194
  93.8 0.0 copy-start.10
  93.8 6.1 %all-to-all-start = ((bf16[16,8,64,256]{3,2,1,0:T(8,128)(2,1)}), bf16[16,8,64,256]{3,2,1,0:T(8,128)(2,1)}, u32[]{:S(2)}, u32[]{:S(2)}) async-start(bf16[16,8,64,256]{3,2,1,0:T(8,128)(2,1)} %broadcast_select_fusion), calls=%async_computation | async-start | bytes 8388608 | tf_op jit(solution)/shard_map/all_to_all | solution.py:195
  99.9 87.1 %all_gather.13 = bf16[16,3,10240]{2,1,0:T(4,128)(2,1)S(1)} all-gather(bf16[2,3,10240]{2,1,0:T(4,128)(2,1)S(1)} %copy.15), channel_id=1, replica_groups=mesh['dp'=8,'fsdp'=16] {'dp'}, dimensions={0}, use_global_device_ids=true | all-gather | bytes 1105920 | tf_op jit(solution)/shard_map/all_gather | solution.py:181
  187.7 0.0 copy-done.5
  187.8 0.0 copy-done.6
  187.8 0.0 copy-done.7
  187.8 0.0 copy-done.9
  187.8 0.0 copy-done.10
  187.8 0.0 copy-start.3
  187.8 2.2 copy-done.3
  190.0 2.2 copy-done.4
  192.2 14.0 %before_scan.1 = (bf16[256,8192]{1,0:T(8,128)(2,1)S(1)}, bf16[256,8192]{1,0:T(8,128)(2,1)S(1)}, f32[256,8192]{1,0:T(8,128)}) custom-call(bf16[256,8192]{1,0:T(8,128)(2,1)S(1)} %copy-done.3, bf16[256,8192]{1,0:T(8,128)(2,1)S(1)} %copy-done.4, f32[256,128]{1,0:T(8,128)S(1)} %copy-done.7, f32[1,128]{1,0:T(1,128)S(1)} %bitcast.18, f32[1,128]{1,0:T(1,128)S(1)} %bitcast.19, ...), custom_call_target="tpu_custom_call" | custom-call | tf_op jit(solution)/shard_map/before_scan/pallas_call | solution.py:82
  206.2 2.1 copy-done
  208.3 1.9 copy-done.2
  210.2 102.1 %all-gather.3.cloned.1.call-done = bf16[8192,2048]{1,0:T(8,128)(2,1)} async-done(((bf16[512,2048]{1,0:T(8,128)(2,1)}), bf16[8192,2048]{1,0:T(8,128)(2,1)}) %all-gather.3.cloned.1.call-update) | async-done | bytes 33554448 | tf_op jit(solution)/shard_map/all_gather | solution.py:191
  312.3 16.2 %fusion.b_ref.c_ref = f32[256,2048]{1,0:T(8,128)S(1)} fusion(bf16[256,8192]{1,0:T(8,128)(2,1)} %param.14, bf16[8192,2048]{1,0:T(8,128)(2,1)} %all-gather.3.cloned.1.call-done), kind=kOutput, calls=%fused_computation.6 | convolution fusion | flops 8589934592 | bytes 39845888 | tf_op jit(solution)/shard_map/dot_general | solution.py:189
  328.5 0.0 all-to-all-done
  328.5 0.0 copy-done.8
  328.5 0.0 copy-start.1
  328.5 2.2 copy-done.1
  330.7 12.8 %scan_and_norm.1 = bf16[256,8192]{1,0:T(8,128)(2,1)} custom-call(s32[1]{0:T(128)S(6)} %copy.18.length_ref, f32[256,2048]{1,0:T(8,128)S(1)} %fusion.b_ref.c_ref, f32[256,2048]{1,0:T(8,128)S(1)} %fusion.b_ref.c_ref, f32[4,10240]{1,0:T(4,128)S(1)} %copy-done.5, f32[4,10240]{1,0:T(4,128)S(1)} %copy-done.5, f32[1,10240]{1,0:T(1,128)S(1)} %bitcast.15, ...), custom_call_target="tpu_custom_call" | custom-call | tf_op jit(solution)/shard_map/scan_and_norm/pallas_call | solution.py:152
  (13 shorter events, 0.1 us)
Async XLA Ops:
  6.5 77.6 %all-gather.5.cloned.1.call-start = ((), (), s32[]{:S(2)}) async-start(), calls=%async_computation.2 | async-start | bytes 4718592 | tf_op jit(solution)/shard_map/all_gather | solution.py:183
  7.3 305.0 %all-gather.3.cloned.1.call-start = ((), (), s32[]{:S(2)}) async-start(), calls=%async_computation.1 | async-start | bytes 35651584 | tf_op jit(solution)/shard_map/all_gather | solution.py:191
  93.8 93.9 %copy-start.5 = (f32[4,10240]{1,0:T(4,128)S(1)}, f32[4,10240]{1,0:T(4,128)}, u32[]{:S(2)}) copy-start(f32[4,10240]{1,0:T(4,128)} %c_taps_ref.1) | copy-start | bytes 491524
  93.8 93.9 %copy-start.6 = (f32[10240]{0:T(1024)S(1)}, f32[10240]{0:T(1024)}, u32[]{:S(2)}) copy-start(f32[10240]{0:T(1024)} %param.20) | copy-start | bytes 122884
  93.8 93.9 %copy-start.7 = (f32[256,128]{1,0:T(8,128)S(1)}, f32[256,128]{1,0:T(8,128)}, u32[]{:S(2)}) copy-start(f32[256,128]{1,0:T(8,128)} %step_ref.1) | copy-start | bytes 393220
  93.8 94.0 %copy-start.9 = (f32[128]{0:T(128)S(1)}, f32[128]{0:T(128)}, u32[]{:S(2)}) copy-start(f32[128]{0:T(128)} %param.21) | copy-start | bytes 1540
  93.8 94.0 %copy-start.10 = (f32[128]{0:T(128)S(1)}, f32[128]{0:T(128)}, u32[]{:S(2)}) copy-start(f32[128]{0:T(128)} %param.22) | copy-start | bytes 1540
  93.8 234.7 %all-to-all-start = ((bf16[16,8,64,256]{3,2,1,0:T(8,128)(2,1)}), bf16[16,8,64,256]{3,2,1,0:T(8,128)(2,1)}, u32[]{:S(2)}, u32[]{:S(2)}) async-start(bf16[16,8,64,256]{3,2,1,0:T(8,128)(2,1)} %broadcast_select_fusion), calls=%async_computation | async-start | bytes 8388608 | tf_op jit(solution)/shard_map/all_to_all | solution.py:195
  187.8 2.2 copy-start.3
  190.0 2.2 copy-start.4
  206.2 2.1 copy-start
  208.3 1.9 copy-start.2
  210.2 118.3 %copy-start.8 = (f32[8192]{0:T(1024)S(1)}, f32[8192]{0:T(1024)}, u32[]{:S(2)}) copy-start(f32[8192]{0:T(1024)} %param.23) | copy-start | bytes 98308
  328.5 2.2 copy-start.1
Sparse Core Ops, SparseCore 0:
  9.7 74.3 all-gather.4
  85.8 226.3 all-gather.2

commit v2 on v1

v2 whole, which is shorter than its diff:
```python
import jax
import jax.numpy as jnp
from jax import lax
from jax.experimental import pallas as pl
from jax.experimental.pallas import tpu as pltpu
from jax.sharding import PartitionSpec as P

F32 = jnp.float32
BF16 = jnp.bfloat16
PIECE = 512
HEAD_ROWS = 16


def split_two(value):
    high = value.astype(BF16)
    return high, (value - high.astype(F32)).astype(BF16)


def dot_nn(left, right):
    return jnp.dot(left, right, preferred_element_type=F32)


def dot_nt(left, right):
    return lax.dot_general(left, right, (((1,), (1,)), ((), ())), preferred_element_type=F32)


def silu(value):
    half = 0.5 * value
    return half + half * jnp.tanh(half)


def convolve(pad_ref, rows, first, taps, bias):
    count = rows.shape[0]
    pad_ref[5:8, :] = first
    pad_ref[8 : 8 + count, :] = rows
    total = taps[3:4, :] * rows + bias
    for k in range(3):
        total = total + taps[k : k + 1, :] * pad_ref[5 + k : 5 + k + count, :]
    return total


def before_kernel(
    inner_ref, gate_ref, step_ref, decay_ref, step_bias_ref, taps_ref, bias_ref,
    high_ref, low_ref, gate_out_ref, factor_ref,
    pad_ref, heads_ref, grow_ref, fall_ref,
):
    tile = pl.program_id(0)
    count = inner_ref.shape[0]
    width = inner_ref.shape[1]
    heads = step_ref.shape[1]

    @pl.when(tile == 0)
    def _():
        raw = step_ref[...] + step_bias_ref[...]
        steps = jnp.maximum(raw, 0.0) + jnp.log1p(jnp.exp(-jnp.abs(raw)))
        logs = -jnp.exp(decay_ref[...]) * steps
        place = lax.broadcasted_iota(jnp.int32, (count, count), 0)
        other = lax.broadcasted_iota(jnp.int32, (count, count), 1)
        lower = jnp.where(place >= other, 1.0, 0.0).astype(BF16)
        top = logs.astype(BF16)
        rest = logs - top.astype(F32)
        mid, last = split_two(rest)
        summed = dot_nn(lower, top) + (dot_nn(lower, mid) + dot_nn(lower, last))
        grow_ref[:, :heads], grow_ref[:, heads:] = split_two(steps * jnp.exp(-summed))
        fall_ref[:, :heads], fall_ref[:, heads:] = split_two(jnp.exp(summed))
        head = lax.broadcasted_iota(jnp.int32, (2 * heads, width), 0)
        column = lax.broadcasted_iota(jnp.int32, (2 * heads, width), 1)
        heads_ref[...] = jnp.where(head >= heads, head - heads, head) - column // 64

    spread = jnp.where(heads_ref[...] == tile * (width // 64), 1.0, 0.0).astype(BF16)
    rows = inner_ref[...].astype(F32)
    factor = dot_nn(grow_ref[...], spread)
    factor_ref[...] = factor[:HEAD_ROWS, :]
    none = jnp.zeros((3, width), F32)
    active = silu(convolve(pad_ref, rows, none, taps_ref[...], bias_ref[...]))
    high_ref[...], low_ref[...] = split_two(active * factor)
    gate_out_ref[...] = silu(gate_ref[...].astype(F32)) * dot_nn(fall_ref[...], spread)


def before(inner_raw, gate_raw, step_raw, decay_log, step_bias, conv_weight, conv_bias):
    count, features = inner_raw.shape
    heads = step_raw.shape[1]
    width = PIECE
    across = lambda rows: pl.BlockSpec((rows, width), lambda j: (0, j))
    whole = lambda rows: pl.BlockSpec((rows, heads), lambda j: (0, 0))
    return pl.pallas_call(
        before_kernel,
        grid=(features // width,),
        in_specs=[
            across(count), across(count), whole(count), whole(1), whole(1),
            across(4), across(1),
        ],
        out_specs=[across(count), across(count), across(count), across(HEAD_ROWS)],
        out_shape=[
            jax.ShapeDtypeStruct((count, features), BF16),
            jax.ShapeDtypeStruct((count, features), BF16),
            jax.ShapeDtypeStruct((count, features), F32),
            jax.ShapeDtypeStruct((HEAD_ROWS, features), F32),
        ],
        scratch_shapes=[
            pltpu.VMEM((count + 8, width), F32),
            pltpu.VMEM((2 * heads, width), jnp.int32),
            pltpu.VMEM((count, 2 * heads), BF16),
            pltpu.VMEM((count, 2 * heads), BF16),
        ],
        compiler_params=pltpu.CompilerParams(vmem_limit_bytes=32 * 2**20),
        name="before_scan",
    )(inner_raw, gate_raw, step_raw, decay_log, step_bias, conv_weight, conv_bias)


def after_kernel(
    length_ref, b_ref, c_ref, b_taps_ref, c_taps_ref, taps_ref, b_bias_ref, c_bias_ref, bias_ref,
    b_first_ref, c_first_ref, first_ref, state_ref, inner_ref, factor_ref,
    high_ref, low_ref, gate_ref, gain_ref, out_ref, pad_ref, head_pad_ref, gated_ref,
):
    count = b_ref.shape[0]
    features = high_ref.shape[1]

    def channel(pad, rows, first, taps, bias):
        return silu(convolve(pad, rows[...].astype(F32), first[...].astype(F32), taps[...], bias[...]))

    head_rows = channel(head_pad_ref, inner_ref, first_ref, taps_ref, bias_ref) * factor_ref[...]
    head_high, head_low = split_two(head_rows)
    b_high, b_low = split_two(channel(pad_ref, b_ref, b_first_ref, b_taps_ref, b_bias_ref))
    c_high, c_low = split_two(channel(pad_ref, c_ref, c_first_ref, c_taps_ref, c_bias_ref))
    scores = dot_nt(c_high, b_high) + (dot_nt(c_high, b_low) + dot_nt(c_low, b_high))
    place = lax.broadcasted_iota(jnp.int32, (count, count), 0)
    other = lax.broadcasted_iota(jnp.int32, (count, count), 1)
    m_high, m_low = split_two(jnp.where(place >= other, scores, 0.0))
    squares = jnp.zeros((count, 128), F32)
    for low in range(0, features, PIECE):
        cols = slice(low, low + PIECE)
        state = state_ref[low // PIECE]
        high = jnp.concatenate([head_high[:, cols], high_ref[HEAD_ROWS:, cols]], axis=0)
        rest = jnp.concatenate([head_low[:, cols], low_ref[HEAD_ROWS:, cols]], axis=0)
        total = dot_nt(c_high, state) + dot_nt(c_low, state)
        total = total + dot_nn(m_high, high)
        total = total + (dot_nn(m_high, rest) + dot_nn(m_low, high))
        gated = total * gate_ref[:, cols]
        gated_ref[:, cols] = gated
        for at in range(0, PIECE, 128):
            part = gated[:, at : at + 128]
            squares = squares + part * part
    mean = jnp.sum(squares, axis=1, keepdims=True) * (1.0 / features)
    row = lax.broadcasted_iota(jnp.int32, (count, 1), 0)
    scale = jnp.where(row < length_ref[0], lax.rsqrt(mean + 1e-05), 0.0)
    for low in range(0, features, PIECE):
        cols = slice(low, low + PIECE)
        out_ref[:, cols] = (gated_ref[:, cols] * scale * gain_ref[:, cols]).astype(BF16)


def after(
    length, projected, conv_weight, conv_bias, conv_rows, state, inner_raw, factor, high, low, gate, norm_gain
):
    count, features = high.shape
    n = state.shape[2]
    groups = projected.shape[1] // (2 * n)
    width = features // groups
    first_b = features // n
    at = lambda rows, base: pl.BlockSpec((rows, n), lambda g, base=base: (0, base + g))
    wide = lambda rows: pl.BlockSpec((rows, width), lambda g: (0, g))
    return pl.pallas_call(
        after_kernel,
        grid=(groups,),
        in_specs=[
            pl.BlockSpec(memory_space=pltpu.SMEM),
            at(count, 0), at(count, groups),
            at(4, first_b), at(4, first_b + groups), wide(4),
            at(1, first_b), at(1, first_b + groups), wide(1),
            at(3, first_b), at(3, first_b + groups), wide(3),
            pl.BlockSpec((width // PIECE, PIECE, n), lambda g: (g, 0, 0)),
            wide(HEAD_ROWS), wide(HEAD_ROWS),
            wide(count), wide(count), wide(count), wide(1),
        ],
        out_specs=wide(count),
        out_shape=jax.ShapeDtypeStruct((count, features), BF16),
        scratch_shapes=[
            pltpu.VMEM((count + 8, n), F32),
            pltpu.VMEM((HEAD_ROWS + 8, width), F32),
            pltpu.VMEM((count, width), F32),
        ],
        compiler_params=pltpu.CompilerParams(vmem_limit_bytes=40 * 2**20),
        name="scan_and_norm",
    )(
        length, projected, projected, conv_weight, conv_weight, conv_weight, conv_bias, conv_bias, conv_bias,
        conv_rows, conv_rows, conv_rows, state, inner_raw, factor, high, low, gate, norm_gain,
    )


EXTRA = 16
QUARTER = 512
MESH = pl.DeviceIdType.MESH


def exchange_kernel(
    prompt_ref, hidden_ref, weight_ref, states_ref, projected_ref, arrived_ref,
    weights, rows, states, outgoing, prompts, prompt_words, partial, total, landed,
    w_send, w_recv, z_send, z_recv, d_send, d_recv, s_send, s_recv, o_send, o_recv,
    p_send, p_recv, h_send, h_recv, t_send, t_recv, local_sem,
):
    dp, fsdp = lax.axis_index("dp"), lax.axis_index("fsdp")
    z, x, core = dp % 4, (fsdp // 2) % 4, fsdp % 2
    y = (dp // 4) * 2 + fsdp // 8
    parity = y % 2
    half_cols = 4096
    count = hidden_ref.shape[0]

    def device(xx, yy, zz, cc):
        xx, yy, zz, cc = xx % 4, yy % 4, zz % 4, cc % 2
        return ((yy // 2) * 4 + zz, ((yy % 2) * 4 + xx) * 2 + cc)

    sibling = device(x, y, z, core + 1)
    x_up, x_down = device(x + 1, y, z, core), device(x + 3, y, z, core)
    z_up, z_down = device(x, y, z + 1, core), device(x, y, z + 3, core)
    across = device(x, y + 2, z, core)
    partner = device(x, y + 1 + 2 * core, z, core + 1)

    def remote(src, dst, send, recv, to):
        return pltpu.make_async_remote_copy(
            src_ref=src, dst_ref=dst, send_sem=send, recv_sem=recv, device_id=to, device_id_type=MESH
        )

    sent = []

    def send(src, dst, send_sem, recv_sem, to):
        copy = remote(src, dst, send_sem, recv_sem, to)
        copy.start()
        sent.append(copy)

    def landing(dst, recv_sem):
        remote(dst, dst, recv_sem, recv_sem, sibling).wait_recv()

    barrier = pltpu.get_barrier_semaphore()

    def greet(to):
        pl.semaphore_signal(barrier, inc=1, device_id=to, device_id_type=MESH)

    for dx in range(4):
        for dc in range(2):
            if dx or dc:
                greet(device(x + dx, y, z, core + dc))
            greet(device(x + dx, y + 1, z, core + dc))
            greet(device(x + dx, y + 3, z, core + dc))
    for to in (z_up, z_down, across):
        greet(to)
    pl.semaphore_wait(barrier, 26)

    me = x * 2 + core
    prompts[0, me] = jnp.full((8, 128), prompt_ref[0], jnp.int32)
    mine = prompts.at[0, me]

    def tell(i, _):
        dx, dc = i // 2, i % 2

        @pl.when(i > 0)
        def _():
            remote(mine, prompts.at[0, me], p_send.at[0, i], p_recv.at[0, me], device(x + dx, y, z, core + dc)).start()

        remote(mine, prompts.at[2, me], p_send.at[1, i], p_recv.at[2, me], device(x + dx, y + 1, z, core + dc)).start()
        remote(mine, prompts.at[1, me], p_send.at[2, i], p_recv.at[1, me], device(x + dx, y + 3, z, core + dc)).start()
        return 0

    lax.fori_loop(0, 8, tell, 0)

    def unit(of):
        return states.at[pl.ds(2 * of, 2)]

    def dp_at(yy, zz):
        return ((yy % 4) // 2) * 4 + zz % 4

    unit_here, unit_across = dp_at(y, z), dp_at(y + 2, z)
    keep_states = pltpu.make_async_copy(states_ref, unit(unit_here), local_sem.at[0])
    keep_states.start()
    send(states_ref, unit(unit_here), s_send.at[0], s_recv.at[0], across)
    send(states_ref, unit(unit_here), s_send.at[1], s_recv.at[1], z_up)
    send(states_ref, unit(unit_here), s_send.at[2], s_recv.at[2], z_down)

    def block(xx, cc):
        return ((xx % 4) * 2 + cc % 2) * 512

    def weight_at(quarter, xx, cc, low=0, many=512):
        return weights.at[quarter % 4, pl.ds(pl.multiple_of(block(xx, cc) + low, 256), many)]

    def own_quarter(quarter):
        return weight_ref.at[:, pl.ds(pl.multiple_of((quarter % 4) * QUARTER, QUARTER), QUARTER)]

    send(own_quarter(z), weight_at(z, x, core), w_send.at[0], w_recv.at[0], x_up)
    send(own_quarter(z), weight_at(z, x, core), w_send.at[1], w_recv.at[1], x_down)
    theirs = pl.ds(pl.multiple_of((1 - parity) * half_cols, half_cols), half_cols)
    ours = pl.ds(pl.multiple_of(parity * half_cols, half_cols), half_cols)
    send(hidden_ref.at[:, theirs], rows.at[pl.ds(0, count)], h_send.at[0], h_recv.at[0], partner)
    keep_rows = pltpu.make_async_copy(hidden_ref.at[:, ours], rows.at[pl.ds(count, count)], local_sem.at[1])
    keep_rows.start()
    keep_weights = []
    for step in range(4):
        at = (0, 1, 3, 2)[step]
        send(own_quarter(z + at), weight_at(z + at, x, core), d_send.at[at], d_recv.at[at], sibling)
        copy = pltpu.make_async_copy(own_quarter(z + at), weight_at(z + at, x, core), local_sem.at[2 + at])
        copy.start()
        keep_weights.append(copy)

    def pass_on(quarter_step, dx, slot):
        whole = weight_at(z + quarter_step, x + dx, core)
        send(whole, whole, d_send.at[slot], d_recv.at[slot], sibling)

    def along_z(dx):
        whole = weight_at(z, x + dx, core)
        at = (3, 1, 2).index(dx)
        send(whole, whole, z_send.at[at], z_recv.at[at], z_up)
        send(whole, whole, z_send.at[3 + at], z_recv.at[3 + at], z_down)

    landing(unit(unit_across), s_recv.at[0])
    send(unit(unit_across), unit(unit_across), s_send.at[3], s_recv.at[3], z_up)
    send(unit(unit_across), unit(unit_across), s_send.at[4], s_recv.at[4], z_down)

    landing(weight_at(z, x + 3, core), w_recv.at[0])
    first = weight_at(z, x + 3, core, 0, 256)
    send(first, first, w_send.at[2], w_recv.at[2], x_up)
    along_z(3)
    pass_on(0, 3, 4)
    landing(weight_at(z, x + 1, core), w_recv.at[1])
    second = weight_at(z, x + 1, core, 256, 256)
    send(second, second, w_send.at[3], w_recv.at[3], x_down)
    along_z(1)
    pass_on(0, 1, 5)

    def state_hop(yy, base, up_slot, down_slot, send_slot):
        below, above = dp_at(yy, z + 3), dp_at(yy, z + 1)
        landing(unit(below), s_recv.at[up_slot])
        one = states.at[2 * below]
        send(one, one, s_send.at[send_slot], s_recv.at[send_slot], z_up)
        landing(unit(above), s_recv.at[down_slot])
        other = states.at[2 * above + 1]
        send(other, other, s_send.at[send_slot + 1], s_recv.at[send_slot + 1], z_down)

    state_hop(y, 0, 1, 2, 5)
    landing(weight_at(z, x + 2, core, 0, 256), w_recv.at[2])
    landing(weight_at(z, x + 2, core, 256, 256), w_recv.at[3])
    along_z(2)
    pass_on(0, 2, 6)
    state_hop(y + 2, 0, 3, 4, 7)

    def multiply(step, slots):
        quarter = (z + step) % 4
        keep_weights[(0, 1, 3, 2).index(step)].wait()
        landing(weight_at(quarter, x, core + 1), d_recv.at[step])
        for dx, slot in zip((3, 1, 2), slots):
            landing(weight_at(quarter, x + dx, core + 1), d_recv.at[slot])

        def columns(n, _):
            cols = pl.ds(pl.multiple_of(n * 256, 256), 256)
            partial[step, :, cols] = dot_nn(rows[:count, :], weights[quarter, :, cols])
            return 0

        lax.fori_loop(0, 2, columns, 0)
        send(partial.at[step], landed.at[step], t_send.at[step], t_recv.at[step], partner)

        def own_columns(n, _):
            cols = pl.ds(pl.multiple_of(n * 256, 256), 256)
            total[step, :, cols] = dot_nn(rows[count:, :], weights[quarter, :, cols])
            return 0

        lax.fori_loop(0, 2, own_columns, 0)

    landing(rows.at[pl.ds(0, count)], h_recv.at[0])
    keep_rows.wait()
    multiply(0, (4, 5, 6))

    keep_states.wait()
    for yy, slot in ((y, 5), (y + 2, 7)):
        far = dp_at(yy, z + 2)
        landing(states.at[2 * far], s_recv.at[slot])
        landing(states.at[2 * far + 1], s_recv.at[slot + 1])

    def heard(i, _):
        @pl.when(i != me)
        def _():
            landing(prompts.at[0, i], p_recv.at[0, i])

        landing(prompts.at[1, i], p_recv.at[1, i])
        landing(prompts.at[2, i], p_recv.at[2, i])
        return 0

    lax.fori_loop(0, 8, heard, 0)
    words = pltpu.make_async_copy(prompts, prompt_words, local_sem.at[6])
    words.start()
    words.wait()
    lows = (0, 0, 256)
    many = (PIECE + EXTRA, 256, 256 + EXTRA)

    def give(i, _):
        dx, dc = i // 2, i % 2
        to_x, to_core = (x + dx) % 4, (core + dc) % 2
        at = to_x * 2 + to_core
        for kind in range(3):
            low, size = lows[kind], many[kind]
            outgoing[i, kind, pl.ds(0, size)] = states[prompt_words[kind, at, 0, 0], pl.ds(low, size)]
            src = outgoing.at[i, kind, pl.ds(0, size)]
            dst = arrived_ref.at[fsdp, pl.ds(low, size)]
            to = device(to_x, y + (0, 1, 3)[kind], z, to_core)
            if kind == 0:
                @pl.when(i > 0)
                def _():
                    remote(src, dst, o_send.at[kind, i], o_recv.at[kind, me], to).start()

                @pl.when(i == 0)
                def _():
                    pltpu.make_async_copy(src, dst, local_sem.at[7]).start()
            else:
                remote(src, dst, o_send.at[kind, i], o_recv.at[kind, me], to).start()
        return 0

    lax.fori_loop(0, 8, give, 0)

    for dx, at in ((3, 0), (1, 1), (2, 2)):
        below = weight_at(z + 3, x + dx, core)
        landing(below, z_recv.at[at])
        one = weight_at(z + 3, x + dx, core, 0, 256)
        send(one, one, z_send.at[6 + at], z_recv.at[6 + at], z_up)
        pass_on(3, dx, 7 + at)
        above = weight_at(z + 1, x + dx, core)
        landing(above, z_recv.at[3 + at])
        other = weight_at(z + 1, x + dx, core, 256, 256)
        send(other, other, z_send.at[9 + at], z_recv.at[9 + at], z_down)
        pass_on(1, dx, 10 + at)
    multiply(1, (10, 11, 12))
    multiply(3, (7, 8, 9))
    for dx, at in ((3, 0), (1, 1), (2, 2)):
        landing(weight_at(z + 2, x + dx, core, 0, 256), z_recv.at[6 + at])
        landing(weight_at(z + 2, x + dx, core, 256, 256), z_recv.at[9 + at])
        pass_on(2, dx, 13 + at)
    multiply(2, (13, 14, 15))

    for step in (0, 1, 3, 2):
        landing(landed.at[step], t_recv.at[step])
        cols = pl.ds(pl.multiple_of(((z + step) % 4) * QUARTER, QUARTER), QUARTER)
        projected_ref[:, cols] = total[step] + landed[step]

    def settle(i, _):
        @pl.when(i != me)
        def _():
            landing(arrived_ref.at[parity * 8 + i], o_recv.at[0, i])

        other = (1 - parity) * 8 + i
        landing(arrived_ref.at[other, pl.ds(0, many[1])], o_recv.at[1, i])
        landing(arrived_ref.at[other, pl.ds(lows[2], many[2])], o_recv.at[2, i])

        @pl.when(i > 0)
        def _():
            remote(mine, mine, p_send.at[0, i], p_recv.at[0, i], sibling).wait_send()
            remote(outgoing.at[i, 0], outgoing.at[i, 0], o_send.at[0, i], o_recv.at[0, i], sibling).wait_send()

        for kind in (1, 2):
            src = outgoing.at[i, kind, pl.ds(0, many[kind])]
            remote(mine, mine, p_send.at[kind, i], p_recv.at[kind, i], sibling).wait_send()
            remote(src, src, o_send.at[kind, i], o_recv.at[kind, i], sibling).wait_send()
        return 0

    lax.fori_loop(0, 8, settle, 0)
    pltpu.make_async_copy(outgoing.at[0, 0], arrived_ref.at[fsdp], local_sem.at[7]).wait()
    for copy in sent:
        copy.wait_send()


def exchange(hidden, weight, states, prompt):
    count = hidden.shape[0]
    columns = weight.shape[1]
    deep = PIECE + EXTRA
    dma = lambda *shape: pltpu.SemaphoreType.DMA(shape)
    anywhere = pl.BlockSpec(memory_space=pl.ANY)
    return pl.pallas_call(
        exchange_kernel,
        in_specs=[pl.BlockSpec(memory_space=pltpu.SMEM), anywhere, anywhere, anywhere],
        out_specs=[pl.BlockSpec(memory_space=pltpu.VMEM), anywhere],
        out_shape=[
            jax.ShapeDtypeStruct((count, columns), F32),
            jax.ShapeDtypeStruct((16, deep, 256), BF16),
        ],
        scratch_shapes=[
            pltpu.VMEM((4, 4096, QUARTER), BF16),
            pltpu.VMEM((2 * count, 4096), BF16),
            pltpu.VMEM((16, deep, 256), BF16),
            pltpu.VMEM((8, 3, deep, 256), BF16),
            pltpu.VMEM((3, 8, 8, 128), jnp.int32),
            pltpu.SMEM((3, 8, 8, 128), jnp.int32),
            pltpu.VMEM((4, count, QUARTER), F32),
            pltpu.VMEM((4, count, QUARTER), F32),
            pltpu.VMEM((4, count, QUARTER), F32),
            dma(4), dma(4), dma(12), dma(12), dma(16), dma(16), dma(9), dma(9), dma(3, 8), dma(3, 8),
            dma(3, 8), dma(3, 8), dma(1), dma(1), dma(4), dma(4), dma(8),
        ],
        compiler_params=pltpu.CompilerParams(
            collective_id=0, has_side_effects=True, vmem_limit_bytes=56 * 2**20
        ),
        cost_estimate=pl.CostEstimate(flops=9 * 10**9, bytes_accessed=2**25, transcendentals=0),
        name="exchange",
    )(prompt, hidden, weight, states)


def on_device(
    hidden, inner_raw, gate_raw, step_raw, proj_weight, conv_weight, conv_bias, decay_log, step_bias,
    norm_gain, ssm_state, conv_state, slot_prompt, slot_len,
):
    conv_bias = conv_bias[None, :]
    part = lax.axis_index("fsdp")
    share = conv_state.shape[2] // 16
    prompts = conv_state.shape[0]
    piece = lax.dynamic_slice_in_dim(conv_state, part * share, share, axis=2).reshape(prompts, 3 * share)
    piece = jnp.pad(piece, ((0, 0), (0, EXTRA * 256 - 3 * share))).reshape(prompts, EXTRA, 256)
    own_states = jnp.concatenate([ssm_state.reshape(prompts, PIECE, 256), piece], axis=1)
    projected, state = exchange(hidden, proj_weight, own_states, slot_prompt)
    conv_rows = state[:, PIECE:, :].reshape(16, EXTRA * 256)[:, : 3 * share].reshape(16, 3, share)
    conv_rows = conv_rows.transpose(1, 0, 2).reshape(3, 16 * share)
    high, low, gate, factor = before(
        inner_raw, gate_raw, step_raw, decay_log[None, :], step_bias[None, :], conv_weight, conv_bias
    )
    return after(
        slot_len, projected, conv_weight, conv_bias, conv_rows, state, inner_raw, factor, high, low, gate,
        norm_gain[None, :],
    )


def solution(mesh):
    rows = P(("dp", "fsdp"), None)
    in_specs = (
        rows, rows, rows, rows, P("fsdp", None), P(), P(), P(), P(), P(),
        P("dp", "fsdp", None, None), P("dp", None, None), P(("dp", "fsdp")), P(("dp", "fsdp")),
    )
    return jax.shard_map(on_device, mesh=mesh, in_specs=in_specs, out_specs=rows, check_vma=False)
```

time: 351 us -> 174 us (0.50)
  waiting for transfers between devices: 165 us -> 0 us
  Pallas kernels: 26.8 us -> 163 us
  blocking collectives: 97.9 us -> 0 us
  matrix products: 16.2 us -> 0 us
  between operations: 14.8 us -> 1.46 us
  local copies, waits for them, and re-layouts: 18.6 us -> 7.37 us
  starting transfers between devices: 6.1 us -> 0 us
    all_gather x2 -> x0, waiting for transfers between devices: 164 us -> none  [the longest x1 102 us: on_device(): lax.all_gather(proj_weight, 'fsdp', axis=0, tiled=True)]
    pallas_call x0 -> x1, Pallas kernels: none -> 137 us  [exchange(): pl.pallas_call(exchange_kernel, in_specs=[pl.BlockSpec(memory_space=pltpu...]
    all_gather x1 -> x0, blocking collectives: 87.1 us -> none  [on_device(): conv_all = lax.all_gather(conv_state, 'dp', axis=0, tiled=True)]
    dot_general x1 -> x0, matrix products: 16.2 us -> none  [on_device(): jnp.dot(hidden, lax.all_gather(proj_weight, 'fsdp', axis=0, tiled=True),...]
    unnamed x1 -> x0, blocking collectives: 10.8 us -> none
    unnamed x26, local copies, waits for them, and re-layouts: 13.6 us -> 6.4 us
    all_to_all x1 -> x0, starting transfers between devices: 6.06 us -> none  [on_device(): lax.all_to_all(outgoing, 'fsdp', split_axis=0, concat_axis=0, tiled=True)]
    gather x1 -> x0, local copies, waits for them, and re-layouts: 5.01 us -> none  [on_device(): outgoing = jnp.take(states, owners, axis=0)]
  transfers between devices with their start and end apart: 3 -> 0, of which waited for: 2 -> 0; matrix products, arithmetic and copies ran while one was open for 8% -> 0% of each run, Pallas kernels for 4% -> 0%
where the time goes in v2:
time: 174 us
  Pallas kernels  163 us (94%)
  local copies, waits for them, and re-layouts  7.37 us (4%)
  other arithmetic  1.88 us (1%)
    pallas_call x1, Pallas kernels, exchange(): pl.pallas_call(exchange_kernel, in_specs=[pl.BlockSpec(memory_space=pltpu...  137 us
    pallas_call x1, Pallas kernels, before(): pl.pallas_call(before_kernel, grid=(features // width,), in_specs=[across...  14 us
    pallas_call x1, Pallas kernels, after(): pl.pallas_call(after_kernel, grid=(groups,), in_specs=[pl.BlockSpec(memor...  12.9 us
    unnamed x26, local copies, waits for them, and re-layouts  6.4 us

profile of v2, /device:TPU:1, one launch (start us, length us, event | category | flops | bytes accessed | tf_op | source)
XLA Modules:
  0.0 174.2 jit_solution(12970696816426286293)
XLA Ops:
  0.0 0.0 copy-start
  1.3 0.0 copy-done
  1.4 1.9 %pad_maximum_fusion.states_ref = bf16[2,528,256]{2,1,0:T(8,128)(2,1)} fusion(bf16[2,16,256]{2,1,0:T(8,128)(2,1)S(1)} %bitcast.28, bf16[2,512,256]{2,1,0:T(8,128)(2,1)} %bitcast.25), kind=kLoop, calls=%fused_computation | loop fusion | flops 1081344 | bytes 1081344 | tf_op jit(solution)/shard_map/concatenate | solution.py:510
  3.3 0.0 copy-start.6
  3.3 0.0 copy-start.7
  3.3 0.0 copy-start.8
  3.3 0.0 copy-start.10
  3.3 0.0 copy-start.11
  3.3 136.6 %exchange.1 = (f32[256,2048]{1,0:T(8,128)}, bf16[16,528,256]{2,1,0:T(8,128)(2,1)}) custom-call(s32[1]{0:T(128)S(6)} %copy.19.prompt_ref, bf16[256,8192]{1,0:T(8,128)(2,1)} %hidden_ref.1, bf16[512,2048]{1,0:T(8,128)(2,1)} %weight_ref.1, bf16[2,528,256]{2,1,0:T(8,128)(2,1)} %pad_maximum_fusion.states_ref), custom_call_target="tpu_custom_call" | custom-call | flops 8999999488 | bytes 33554432 | tf_op jit(solution)/shard_map/exchange/pallas_call | solution.py:471
  139.9 0.9 slice.6
  140.9 0.0 copy-done.6
  140.9 0.0 copy-done.7
  140.9 0.0 copy-done.8
  141.0 0.0 copy-done.10
  141.0 0.0 copy-done.11
  141.0 0.0 copy-start.1
  141.0 2.2 %copy-done.1 = bf16[256,8192]{1,0:T(8,128)(2,1)S(1)} copy-done((bf16[256,8192]{1,0:T(8,128)(2,1)S(1)}, bf16[256,8192]{1,0:T(8,128)(2,1)}, u32[]{:S(2)}) %copy-start.1) | copy-done | bytes 4194328
  143.2 0.0 copy-start.5
  143.2 2.2 %copy-done.5 = bf16[256,8192]{1,0:T(8,128)(2,1)S(1)} copy-done((bf16[256,8192]{1,0:T(8,128)(2,1)S(1)}, bf16[256,8192]{1,0:T(8,128)(2,1)}, u32[]{:S(2)}) %copy-start.5) | copy-done | bytes 4194328
  145.4 0.0 copy-start.2
  145.4 0.0 copy-start.3
  145.4 0.0 copy-start.9
  145.4 14.0 %before_scan.1 = (bf16[256,8192]{1,0:T(8,128)(2,1)S(1)}, bf16[256,8192]{1,0:T(8,128)(2,1)S(1)}, f32[256,8192]{1,0:T(8,128)}, f32[16,8192]{1,0:T(8,128)S(1)}) custom-call(bf16[256,8192]{1,0:T(8,128)(2,1)S(1)} %copy-done.1, bf16[256,8192]{1,0:T(8,128)(2,1)S(1)} %copy-done.5, f32[256,128]{1,0:T(8,128)S(1)} %copy-done.8, f32[1,128]{1,0:T(1,128)S(1)} %bitcast.23, ...), custom_call_target="tpu_custom_call" | custom-call | tf_op jit(solution)/shard_map/before_scan/pallas_call | solution.py:86
  159.4 0.0 copy-start.4
  159.4 1.9 %copy-done.4 = bf16[256,8192]{1,0:T(8,128)(2,1)} copy-done((bf16[256,8192]{1,0:T(8,128)(2,1)}, bf16[256,8192]{1,0:T(8,128)(2,1)S(1)}, u32[]{:S(2)}) %copy-start.4) | copy-done | bytes 4194328
  161.3 0.0 copy-done.2
  161.3 0.0 copy-done.3
  161.3 0.0 copy-done.9
  161.3 12.9 %scan_and_norm.1 = bf16[256,8192]{1,0:T(8,128)(2,1)} custom-call(s32[1]{0:T(128)S(6)} %copy.20.length_ref, f32[256,2048]{1,0:T(8,128)S(1)} %copy-done.3, f32[256,2048]{1,0:T(8,128)S(1)} %copy-done.3, f32[4,10240]{1,0:T(4,128)S(1)} %copy-done.6, f32[4,10240]{1,0:T(4,128)S(1)} %copy-done.6, f32[4,10240]{1,0:T(4,128)S(1)} %copy-done.6, ...), custom_call_target="tpu_custom_call" | custom-call | tf_op jit(solution)/shard_map/scan_and_norm/pallas_call | solution.py:162
  (6 shorter events, 0.1 us)
Async XLA Ops:
  0.0 1.3 copy-start
  3.3 137.6 %copy-start.6 = (f32[4,10240]{1,0:T(4,128)S(1)}, f32[4,10240]{1,0:T(4,128)}, u32[]{:S(2)}) copy-start(f32[4,10240]{1,0:T(4,128)} %taps_ref.3) | copy-start | bytes 491524
  3.3 137.7 %copy-start.7 = (f32[10240]{0:T(1024)S(1)}, f32[10240]{0:T(1024)}, u32[]{:S(2)}) copy-start(f32[10240]{0:T(1024)} %param.20) | copy-start | bytes 122884
  3.3 137.7 %copy-start.8 = (f32[256,128]{1,0:T(8,128)S(1)}, f32[256,128]{1,0:T(8,128)}, u32[]{:S(2)}) copy-start(f32[256,128]{1,0:T(8,128)} %step_ref.1) | copy-start | bytes 393220
  3.3 137.7 %copy-start.10 = (f32[128]{0:T(128)S(1)}, f32[128]{0:T(128)}, u32[]{:S(2)}) copy-start(f32[128]{0:T(128)} %param.21) | copy-start | bytes 1540
  3.3 137.7 %copy-start.11 = (f32[128]{0:T(128)S(1)}, f32[128]{0:T(128)}, u32[]{:S(2)}) copy-start(f32[128]{0:T(128)} %param.22) | copy-start | bytes 1540
  141.0 2.2 %copy-start.1 = (bf16[256,8192]{1,0:T(8,128)(2,1)S(1)}, bf16[256,8192]{1,0:T(8,128)(2,1)}, u32[]{:S(2)}) copy-start(bf16[256,8192]{1,0:T(8,128)(2,1)} %inner_ref.3) | copy-start | bytes 12582916
  143.2 2.2 %copy-start.5 = (bf16[256,8192]{1,0:T(8,128)(2,1)S(1)}, bf16[256,8192]{1,0:T(8,128)(2,1)}, u32[]{:S(2)}) copy-start(bf16[256,8192]{1,0:T(8,128)(2,1)} %gate_ref.1) | copy-start | bytes 12582916
  145.4 15.9 %copy-start.2 = (bf16[256,8192]{1,0:T(8,128)(2,1)S(1)}, bf16[256,8192]{1,0:T(8,128)(2,1)}, u32[]{:S(2)}) copy-start(bf16[256,8192]{1,0:T(8,128)(2,1)} %inner_ref.3) | copy-start | bytes 12582916
  145.4 15.9 %copy-start.3 = (f32[256,2048]{1,0:T(8,128)S(1)}, f32[256,2048]{1,0:T(8,128)}, u32[]{:S(2)}) copy-start(f32[256,2048]{1,0:T(8,128)} %get-tuple-element.11.b_ref.c_ref) | copy-start | bytes 6291460
  145.4 15.9 %copy-start.9 = (f32[8192]{0:T(1024)S(1)}, f32[8192]{0:T(1024)}, u32[]{:S(2)}) copy-start(f32[8192]{0:T(1024)} %param.23) | copy-start | bytes 98308
  159.4 1.9 %copy-start.4 = (bf16[256,8192]{1,0:T(8,128)(2,1)}, bf16[256,8192]{1,0:T(8,128)(2,1)S(1)}, u32[]{:S(2)}) copy-start(bf16[256,8192]{1,0:T(8,128)(2,1)S(1)} %get-tuple-element.15.low_ref) | copy-start | bytes 12582916

commit v3 on v1

v3 whole, which is shorter than its diff:
```python
import jax
import jax.numpy as jnp
from jax import lax
from jax.experimental import pallas as pl
from jax.experimental.pallas import tpu as pltpu
from jax.sharding import PartitionSpec as P

F32 = jnp.float32
BF16 = jnp.bfloat16
PIECE = 512
HEAD_ROWS = 16


def split_two(value):
    high = value.astype(BF16)
    return high, (value - high.astype(F32)).astype(BF16)


def dot_nn(left, right):
    return jnp.dot(left, right, preferred_element_type=F32)


def dot_nt(left, right):
    return lax.dot_general(left, right, (((1,), (1,)), ((), ())), preferred_element_type=F32)


def silu(value):
    half = 0.5 * value
    return half + half * jnp.tanh(half)


def convolve(pad_ref, rows, first, taps, bias):
    count = rows.shape[0]
    pad_ref[5:8, :] = first
    pad_ref[8 : 8 + count, :] = rows
    total = taps[3:4, :] * rows + bias
    for k in range(3):
        total = total + taps[k : k + 1, :] * pad_ref[5 + k : 5 + k + count, :]
    return total


def after_kernel(
    length_ref, b_ref, c_ref, b_taps_ref, c_taps_ref, taps_ref, b_bias_ref, c_bias_ref, bias_ref,
    b_first_ref, c_first_ref, first_ref, state_ref, inner_ref, factor_ref,
    high_ref, low_ref, gate_ref, gain_ref, out_ref, pad_ref, head_pad_ref, gated_ref,
):
    count = b_ref.shape[0]
    features = high_ref.shape[1]

    def channel(pad, rows, first, taps, bias):
        return silu(convolve(pad, rows[...].astype(F32), first[...].astype(F32), taps[...], bias[...]))

    head_rows = channel(head_pad_ref, inner_ref, first_ref, taps_ref, bias_ref) * factor_ref[...]
    head_high, head_low = split_two(head_rows)
    b_high, b_low = split_two(channel(pad_ref, b_ref, b_first_ref, b_taps_ref, b_bias_ref))
    c_high, c_low = split_two(channel(pad_ref, c_ref, c_first_ref, c_taps_ref, c_bias_ref))
    scores = dot_nt(c_high, b_high) + (dot_nt(c_high, b_low) + dot_nt(c_low, b_high))
    place = lax.broadcasted_iota(jnp.int32, (count, count), 0)
    other = lax.broadcasted_iota(jnp.int32, (count, count), 1)
    m_high, m_low = split_two(jnp.where(place >= other, scores, 0.0))
    squares = jnp.zeros((count, 128), F32)
    for low in range(0, features, PIECE):
        cols = slice(low, low + PIECE)
        state = state_ref[low // PIECE]
        high = jnp.concatenate([head_high[:, cols], high_ref[HEAD_ROWS:, cols]], axis=0)
        rest = jnp.concatenate([head_low[:, cols], low_ref[HEAD_ROWS:, cols]], axis=0)
        total = dot_nt(c_high, state) + dot_nt(c_low, state)
        total = total + dot_nn(m_high, high)
        total = total + (dot_nn(m_high, rest) + dot_nn(m_low, high))
        gated = total * gate_ref[:, cols]
        gated_ref[:, cols] = gated
        for at in range(0, PIECE, 128):
            part = gated[:, at : at + 128]
            squares = squares + part * part
    mean = jnp.sum(squares, axis=1, keepdims=True) * (1.0 / features)
    row = lax.broadcasted_iota(jnp.int32, (count, 1), 0)
    scale = jnp.where(row < length_ref[0], lax.rsqrt(mean + 1e-05), 0.0)
    for low in range(0, features, PIECE):
        cols = slice(low, low + PIECE)
        out_ref[:, cols] = (gated_ref[:, cols] * scale * gain_ref[:, cols]).astype(BF16)


def after(
    length, projected, conv_weight, conv_bias, conv_rows, state, inner_raw, factor, high, low, gate, norm_gain
):
    count, features = high.shape
    n = state.shape[2]
    groups = projected.shape[1] // (2 * n)
    width = features // groups
    first_b = features // n
    at = lambda rows, base: pl.BlockSpec((rows, n), lambda g, base=base: (0, base + g))
    wide = lambda rows: pl.BlockSpec((rows, width), lambda g: (0, g))
    return pl.pallas_call(
        after_kernel,
        grid=(groups,),
        in_specs=[
            pl.BlockSpec(memory_space=pltpu.SMEM),
            at(count, 0), at(count, groups),
            at(4, first_b), at(4, first_b + groups), wide(4),
            at(1, first_b), at(1, first_b + groups), wide(1),
            at(3, first_b), at(3, first_b + groups), wide(3),
            pl.BlockSpec((width // PIECE, PIECE, n), lambda g: (g, 0, 0)),
            wide(HEAD_ROWS), wide(HEAD_ROWS),
            wide(count), wide(count), wide(count), wide(1),
        ],
        out_specs=wide(count),
        out_shape=jax.ShapeDtypeStruct((count, features), BF16),
        scratch_shapes=[
            pltpu.VMEM((count + 8, n), F32),
            pltpu.VMEM((HEAD_ROWS + 8, width), F32),
            pltpu.VMEM((count, width), F32),
        ],
        compiler_params=pltpu.CompilerParams(vmem_limit_bytes=62 * 2**20),
        name="scan_and_norm",
    )(
        length, projected, projected, conv_weight, conv_weight, conv_weight, conv_bias, conv_bias, conv_bias,
        conv_rows, conv_rows, conv_rows, state, inner_raw, factor, high, low, gate, norm_gain,
    )


EXTRA = 16
DIRECT = 512
SHARED = 384
MESH = pl.DeviceIdType.MESH
FAR = (3, 1, 2)
HALVES = ((0, 256), (256, 256 + EXTRA))
SPANS = (HALVES, ((0, 128), (256, 128)), ((128, 128), (384, 128 + EXTRA)))


def exchange_kernel(
    prompt_ref, hidden_ref, weight_ref, states_ref, inner_ref, gate_ref, step_ref, decay_ref,
    step_bias_ref, taps_ref, bias_ref,
    projected_ref, arrived_ref, high_ref, low_ref, gate_out_ref, factor_ref,
    shared, direct, rows, states_a, states_b, outgoing, prompts, prompt_words, partial, total, landed,
    partial_d, total_d, landed_d, inner, gate, gate_out, pad_ref, heads_ref, grow_ref, fall_ref,
    w_send, w_recv, x_send, x_recv, z_send, z_recv, d_send, d_recv, s_send, s_recv, o_send, o_recv,
    p_send, p_recv, h_send, h_recv, t_send, t_recv, local_sem,
):
    dp, fsdp = lax.axis_index("dp"), lax.axis_index("fsdp")
    z, x, core = dp % 4, (fsdp // 2) % 4, fsdp % 2
    y = (dp // 4) * 2 + fsdp // 8
    parity = y % 2
    depth = rows.shape[1]
    count = hidden_ref.shape[0]

    def device(xx, yy, zz, cc):
        xx, yy, zz, cc = xx % 4, yy % 4, zz % 4, cc % 2
        return ((yy // 2) * 4 + zz, ((yy % 2) * 4 + xx) * 2 + cc)

    sibling = device(x, y, z, core + 1)
    x_up, x_down = device(x + 1, y, z, core), device(x + 3, y, z, core)
    z_up, z_down = device(x, y, z + 1, core), device(x, y, z + 3, core)
    across = device(x, y + 2, z, core)
    partner = device(x, y + 1 + 2 * core, z, core + 1)

    def remote(src, dst, send, recv, to):
        return pltpu.make_async_remote_copy(
            src_ref=src, dst_ref=dst, send_sem=send, recv_sem=recv, device_id=to, device_id_type=MESH
        )

    sent = []

    def send(src, dst, send_sem, recv_sem, to):
        copy = remote(src, dst, send_sem, recv_sem, to)
        copy.start()
        sent.append(copy)

    def landing(dst, recv_sem):
        remote(dst, dst, recv_sem, recv_sem, sibling).wait_recv()

    def local(src, dst, at):
        copy = pltpu.make_async_copy(src, dst, local_sem.at[at])
        copy.start()
        return copy

    barrier = pltpu.get_barrier_semaphore()

    def greet(to):
        pl.semaphore_signal(barrier, inc=1, device_id=to, device_id_type=MESH)

    for dx in range(4):
        for dc in range(2):
            if dx or dc:
                greet(device(x + dx, y, z, core + dc))
            greet(device(x + dx, y + 1, z, core + dc))
            greet(device(x + dx, y + 3, z, core + dc))
    for to in (z_up, z_down, across):
        greet(to)
    keep_inner = local(inner_ref, inner, 0)
    keep_gate = local(gate_ref, gate, 1)
    me = x * 2 + core
    prompts[0, me] = jnp.full((8, 128), prompt_ref[0], jnp.int32)
    mine = prompts.at[0, me]
    pl.semaphore_wait(barrier, 26)

    states = (states_a, states_b)

    def unit(of, half):
        return states[half].at[pl.ds(2 * of, 2)]

    def one(of, which, half):
        return states[half].at[2 * of + which]

    def dp_at(yy, zz):
        return ((yy % 4) // 2) * 4 + zz % 4

    unit_here, unit_across = dp_at(y, z), dp_at(y + 2, z)

    def own_states(half, slot, to):
        src = states_ref.at[:, pl.ds(*HALVES[half])]
        send(src, unit(unit_here, half), s_send.at[half, slot], s_recv.at[half, slot], to)

    def own_along(half):
        own_states(half, 1, z_up)
        own_states(half, 2, z_down)

    def across_along(half):
        there = unit(unit_across, half)
        landing(there, s_recv.at[half, 0])
        send(there, there, s_send.at[half, 3], s_recv.at[half, 3], z_up)
        send(there, there, s_send.at[half, 4], s_recv.at[half, 4], z_down)

    def hop(half, yy, slot, onward):
        below, above = dp_at(yy, z + 3), dp_at(yy, z + 1)
        landing(unit(below, half), s_recv.at[half, slot])
        first = one(below, 0, half)
        send(first, first, s_send.at[half, onward], s_recv.at[half, onward], z_up)
        landing(unit(above, half), s_recv.at[half, slot + 1])
        second = one(above, 1, half)
        send(second, second, s_send.at[half, onward + 1], s_recv.at[half, onward + 1], z_down)

    def far_states(half):
        for yy, slot in ((y, 5), (y + 2, 7)):
            far = dp_at(yy, z + 2)
            landing(one(far, 0, half), s_recv.at[half, slot])
            landing(one(far, 1, half), s_recv.at[half, slot + 1])

    def block(xx, cc, low):
        return pl.multiple_of(((xx % 4) * 2 + cc % 2) * 512 + low, 256)

    def shared_at(step, xx, cc, low=0, many=512):
        return shared.at[(z + step) % 4, pl.ds(block(xx, cc, low), many)]

    def direct_at(xx, cc, low=0, many=512):
        return direct.at[pl.ds(block(xx, cc, low), many)]

    def own_shared(step):
        low = DIRECT + ((z + step) % 4) * SHARED
        return weight_ref.at[:, pl.ds(pl.multiple_of(low, 128), SHARED)]

    own_direct = weight_ref.at[:, pl.ds(0, DIRECT)]

    def to_sibling(ref, slot):
        send(ref, ref, d_send.at[slot], d_recv.at[slot], sibling)

    def along_z(at):
        whole = shared_at(0, x + FAR[at], core)
        send(whole, whole, z_send.at[at], z_recv.at[at], z_up)
        send(whole, whole, z_send.at[3 + at], z_recv.at[3 + at], z_down)

    def tell(i, _):
        dx, dc = i // 2, i % 2

        @pl.when(i > 0)
        def _():
            remote(mine, mine, p_send.at[0, i], p_recv.at[0, me], device(x + dx, y, z, core + dc)).start()

        remote(mine, prompts.at[2, me], p_send.at[1, i], p_recv.at[2, me], device(x + dx, y + 1, z, core + dc)).start()
        remote(mine, prompts.at[1, me], p_send.at[2, i], p_recv.at[1, me], device(x + dx, y + 3, z, core + dc)).start()
        return 0

    own_states(0, 0, across)
    own_along(0)
    send(own_shared(0), shared_at(0, x, core), w_send.at[0], w_recv.at[0], x_up)
    send(own_shared(0), shared_at(0, x, core), w_send.at[1], w_recv.at[1], x_down)
    lax.fori_loop(0, 8, tell, 0)
    keep_states = [
        local(states_ref.at[:, pl.ds(*HALVES[half])], unit(unit_here, half), (2, 15)[half]) for half in range(2)
    ]
    theirs = pl.ds(pl.multiple_of((1 - parity) * depth, depth), depth)
    ours = pl.ds(pl.multiple_of(parity * depth, depth), depth)
    keep_rows = local(hidden_ref.at[:, ours], rows.at[pl.ds(count, count)], 3)
    keep = {}
    for step in (0, 1, 3, 2):
        send(own_shared(step), shared_at(step, x, core), d_send.at[step], d_recv.at[step], sibling)
        keep[step] = local(own_shared(step), shared_at(step, x, core), 4 + step)
    send(own_direct, direct_at(x, core), d_send.at[4], d_recv.at[4], sibling)
    keep_direct = local(own_direct, direct_at(x, core), 8)

    heads = step_ref.shape[1]

    def decays():
        raw = step_ref[...] + step_bias_ref[...]
        steps = jnp.maximum(raw, 0.0) + jnp.log1p(jnp.exp(-jnp.abs(raw)))
        logs = -jnp.exp(decay_ref[...]) * steps
        place = lax.broadcasted_iota(jnp.int32, (count, count), 0)
        other = lax.broadcasted_iota(jnp.int32, (count, count), 1)
        lower = jnp.where(place >= other, 1.0, 0.0).astype(BF16)
        top = logs.astype(BF16)
        mid, last = split_two(logs - top.astype(F32))
        summed = dot_nn(lower, top) + (dot_nn(lower, mid) + dot_nn(lower, last))
        grow_ref[:, :heads], grow_ref[:, heads:] = split_two(steps * jnp.exp(-summed))
        fall_ref[:, :heads], fall_ref[:, heads:] = split_two(jnp.exp(summed))
        head = lax.broadcasted_iota(jnp.int32, (2 * heads, PIECE), 0)
        column = lax.broadcasted_iota(jnp.int32, (2 * heads, PIECE), 1)
        heads_ref[...] = jnp.where(head >= heads, head - heads, head) - column // 64

    def prepare(tile, _):
        cols = pl.ds(pl.multiple_of(tile * PIECE, PIECE), PIECE)
        spread = jnp.where(heads_ref[...] == tile * (PIECE // 64), 1.0, 0.0).astype(BF16)
        factor = dot_nn(grow_ref[...], spread)
        factor_ref[:, cols] = factor[:HEAD_ROWS, :]
        none = jnp.zeros((3, PIECE), F32)
        active = silu(convolve(pad_ref, inner[:, cols].astype(F32), none, taps_ref[:, cols], bias_ref[:, cols]))
        gate_out[:, cols] = silu(gate[:, cols].astype(F32)) * dot_nn(fall_ref[...], spread)
        inner[:, cols], gate[:, cols] = split_two(active * factor)
        return 0

    keep_inner.wait()
    keep_gate.wait()
    decays()
    lax.fori_loop(0, 3, prepare, 0)

    across_along(0)
    own_states(1, 0, across)
    hop(0, y, 1, 5)
    landing(shared_at(0, x + 3, core), w_recv.at[0])
    first = shared_at(0, x + 3, core, 0, 256)
    send(first, first, w_send.at[2], w_recv.at[2], x_up)
    to_sibling(shared_at(0, x + 3, core), 5)
    landing(shared_at(0, x + 1, core), w_recv.at[1])
    second = shared_at(0, x + 1, core, 256, 256)
    send(second, second, w_send.at[3], w_recv.at[3], x_down)
    to_sibling(shared_at(0, x + 1, core), 6)
    send(own_direct, direct_at(x, core), x_send.at[0], x_recv.at[0], x_up)
    send(own_direct, direct_at(x, core), x_send.at[1], x_recv.at[1], x_down)
    hop(0, y + 2, 3, 7)
    own_along(1)
    across_along(1)
    send(hidden_ref.at[:, theirs], rows.at[pl.ds(0, count)], h_send.at[0], h_recv.at[0], partner)

    def heard(i, _):
        @pl.when(i != me)
        def _():
            landing(prompts.at[0, i], p_recv.at[0, i])

        landing(prompts.at[1, i], p_recv.at[1, i])
        landing(prompts.at[2, i], p_recv.at[2, i])
        return 0

    def give(half):
        def step(i, _):
            to_x, to_core = (x + i // 2) % 4, (core + i % 2) % 2
            at = to_x * 2 + to_core
            for kind in range(3):
                low, size = SPANS[kind][half]
                span = pl.ds(low, size)
                outgoing[min(kind, 1), i, span] = states[half][
                    prompt_words[kind, at, 0, 0], pl.ds(low - HALVES[half][0], size)
                ]
                src = outgoing.at[min(kind, 1), i, span]
                dst = arrived_ref.at[fsdp, span]
                copy = remote(
                    src, dst, o_send.at[half, kind, i], o_recv.at[half, kind, me],
                    device(to_x, y + (0, 1, 3)[kind], z, to_core),
                )
                if kind == 0:
                    pl.when(i > 0)(copy.start)

                    @pl.when(i == 0)
                    def _():
                        pltpu.make_async_copy(src, dst, local_sem.at[9 + half]).start()
                else:
                    copy.start()
            return 0

        lax.fori_loop(0, 8, step, 0)

    for copy in keep_states:
        copy.wait()
    lax.fori_loop(0, 8, heard, 0)
    local(prompts, prompt_words, 11).wait()
    far_states(0)
    give(0)
    hop(1, y, 1, 5)
    landing(shared_at(0, x + 2, core, 0, 256), w_recv.at[2])
    landing(shared_at(0, x + 2, core, 256, 256), w_recv.at[3])
    to_sibling(shared_at(0, x + 2, core), 7)
    hop(1, y + 2, 3, 7)
    landing(direct_at(x + 3, core), x_recv.at[0])
    first = direct_at(x + 3, core, 0, 256)
    send(first, first, x_send.at[2], x_recv.at[2], x_up)
    to_sibling(direct_at(x + 3, core), 8)
    landing(direct_at(x + 1, core), x_recv.at[1])
    second = direct_at(x + 1, core, 256, 256)
    send(second, second, x_send.at[3], x_recv.at[3], x_down)
    to_sibling(direct_at(x + 1, core), 9)
    lax.fori_loop(3, 6, prepare, 0)
    far_states(1)
    give(1)
    for at in range(3):
        along_z(at)

    def multiply(weights_of, mine_to, theirs_to, theirs_in, slot):
        theirs_to[...] = dot_nn(rows[:count, :], weights_of[...])
        send(theirs_to, theirs_in, t_send.at[slot], t_recv.at[slot], partner)
        mine_to[...] = dot_nn(rows[count:, :], weights_of[...])

    def multiply_shared(step, slots):
        keep[step].wait()
        landing(shared_at(step, x, core + 1), d_recv.at[step])
        for dx, slot in zip(FAR, slots):
            landing(shared_at(step, x + dx, core + 1), d_recv.at[slot])
        multiply(shared.at[(z + step) % 4], total.at[step], partial.at[step], landed.at[step], step)

    landing(rows.at[pl.ds(0, count)], h_recv.at[0])
    keep_rows.wait()
    multiply_shared(0, (5, 6, 7))
    landing(direct_at(x + 2, core, 0, 256), x_recv.at[2])
    landing(direct_at(x + 2, core, 256, 256), x_recv.at[3])
    to_sibling(direct_at(x + 2, core), 10)
    lax.fori_loop(6, 8, prepare, 0)

    for at, dx in enumerate(FAR):
        landing(shared_at(3, x + dx, core), z_recv.at[at])
        first = shared_at(3, x + dx, core, 0, 256)
        send(first, first, z_send.at[6 + at], z_recv.at[6 + at], z_up)
        to_sibling(shared_at(3, x + dx, core), 11 + at)
        landing(shared_at(1, x + dx, core), z_recv.at[3 + at])
        second = shared_at(1, x + dx, core, 256, 256)
        send(second, second, z_send.at[9 + at], z_recv.at[9 + at], z_down)
        to_sibling(shared_at(1, x + dx, core), 14 + at)
        if at == 0:
            keep_direct.wait()
            landing(direct_at(x, core + 1), d_recv.at[4])
            for more, slot in zip(FAR, (8, 9, 10)):
                landing(direct_at(x + more, core + 1), d_recv.at[slot])
            multiply(direct, total_d, partial_d, landed_d, 4)
            lax.fori_loop(8, 11, prepare, 0)
        if at == 1:
            lax.fori_loop(11, 16, prepare, 0)
            leave = [local(inner, high_ref, 12), local(gate, low_ref, 13), local(gate_out, gate_out_ref, 14)]
    multiply_shared(3, (11, 12, 13))
    multiply_shared(1, (14, 15, 16))
    for at, dx in enumerate(FAR):
        landing(shared_at(2, x + dx, core, 0, 256), z_recv.at[6 + at])
        landing(shared_at(2, x + dx, core, 256, 256), z_recv.at[9 + at])
        to_sibling(shared_at(2, x + dx, core), 17 + at)
    multiply_shared(2, (17, 18, 19))

    landing(landed_d, t_recv.at[4])
    projected_ref[:, :DIRECT] = total_d[...] + landed_d[...]
    for step in (0, 3, 1, 2):
        landing(landed.at[step], t_recv.at[step])
        cols = pl.ds(pl.multiple_of(DIRECT + ((z + step) % 4) * SHARED, 128), SHARED)
        projected_ref[:, cols] = total[step] + landed[step]

    def settle(i, _):
        for half in range(2):
            @pl.when(i != me)
            def _():
                landing(arrived_ref.at[parity * 8 + i, pl.ds(*SPANS[0][half])], o_recv.at[half, 0, i])

            for kind in (1, 2):
                landing(arrived_ref.at[(1 - parity) * 8 + i, pl.ds(*SPANS[kind][half])], o_recv.at[half, kind, i])
            for kind in range(3):
                src = outgoing.at[min(kind, 1), i, pl.ds(*SPANS[kind][half])]
                copy = remote(src, src, o_send.at[half, kind, i], o_recv.at[half, kind, i], sibling)
                if kind == 0:
                    pl.when(i > 0)(copy.wait_send)
                else:
                    copy.wait_send()
        for kind in range(3):
            copy = remote(mine, mine, p_send.at[kind, i], p_recv.at[kind, i], sibling)
            if kind == 0:
                pl.when(i > 0)(copy.wait_send)
            else:
                copy.wait_send()
        return 0

    lax.fori_loop(0, 8, settle, 0)
    for half in range(2):
        span = pl.ds(*HALVES[half])
        pltpu.make_async_copy(outgoing.at[0, 0, span], arrived_ref.at[fsdp, span], local_sem.at[9 + half]).wait()
    for copy in leave:
        copy.wait()
    for copy in sent:
        copy.wait_send()


def exchange(
    hidden, weight, states, prompt, inner_raw, gate_raw, step_raw, decay_log, step_bias, conv_weight, conv_bias
):
    count, features = inner_raw.shape
    columns = weight.shape[1]
    heads = step_raw.shape[1]
    deep = PIECE + EXTRA
    dma = lambda *shape: pltpu.SemaphoreType.DMA(shape)
    anywhere = pl.BlockSpec(memory_space=pl.ANY)
    inside = pl.BlockSpec(memory_space=pltpu.VMEM)
    return pl.pallas_call(
        exchange_kernel,
        in_specs=[pl.BlockSpec(memory_space=pltpu.SMEM)] + [anywhere] * 5 + [inside] * 5,
        out_specs=[inside, anywhere, anywhere, anywhere, anywhere, inside],
        out_shape=[
            jax.ShapeDtypeStruct((count, columns), F32),
            jax.ShapeDtypeStruct((16, deep, 256), BF16),
            jax.ShapeDtypeStruct((count, features), BF16),
            jax.ShapeDtypeStruct((count, features), BF16),
            jax.ShapeDtypeStruct((count, features), F32),
            jax.ShapeDtypeStruct((HEAD_ROWS, features), F32),
        ],
        scratch_shapes=[
            pltpu.VMEM((4, 4096, SHARED), BF16),
            pltpu.VMEM((4096, DIRECT), BF16),
            pltpu.VMEM((2 * count, 4096), BF16),
            pltpu.VMEM((16, HALVES[0][1], 256), BF16),
            pltpu.VMEM((16, HALVES[1][1], 256), BF16),
            pltpu.VMEM((2, 8, deep, 256), BF16),
            pltpu.VMEM((3, 8, 8, 128), jnp.int32),
            pltpu.SMEM((3, 8, 8, 128), jnp.int32),
            pltpu.VMEM((4, count, SHARED), F32),
            pltpu.VMEM((4, count, SHARED), F32),
            pltpu.VMEM((4, count, SHARED), F32),
            pltpu.VMEM((count, DIRECT), F32),
            pltpu.VMEM((count, DIRECT), F32),
            pltpu.VMEM((count, DIRECT), F32),
            pltpu.VMEM((count, features), BF16),
            pltpu.VMEM((count, features), BF16),
            pltpu.VMEM((count, features), F32),
            pltpu.VMEM((count + 8, PIECE), F32),
            pltpu.VMEM((2 * heads, PIECE), jnp.int32),
            pltpu.VMEM((count, 2 * heads), BF16),
            pltpu.VMEM((count, 2 * heads), BF16),
            dma(4), dma(4), dma(4), dma(4), dma(12), dma(12), dma(20), dma(20), dma(2, 9), dma(2, 9),
            dma(2, 3, 8), dma(2, 3, 8), dma(3, 8), dma(3, 8), dma(1), dma(1), dma(5), dma(5), dma(16),
        ],
        compiler_params=pltpu.CompilerParams(
            collective_id=0, has_side_effects=True, vmem_limit_bytes=62 * 2**20
        ),
        cost_estimate=pl.CostEstimate(flops=9 * 10**9, bytes_accessed=2**25, transcendentals=0),
        name="exchange",
    )(prompt, hidden, weight, states, inner_raw, gate_raw, step_raw, decay_log, step_bias, conv_weight, conv_bias)


def on_device(
    hidden, inner_raw, gate_raw, step_raw, proj_weight, conv_weight, conv_bias, decay_log, step_bias,
    norm_gain, ssm_state, conv_state, slot_prompt, slot_len,
):
    conv_bias = conv_bias[None, :]
    part = lax.axis_index("fsdp")
    share = conv_state.shape[2] // 16
    prompts = conv_state.shape[0]
    piece = lax.dynamic_slice_in_dim(conv_state, part * share, share, axis=2).reshape(prompts, 3 * share)
    piece = jnp.pad(piece, ((0, 0), (0, EXTRA * 256 - 3 * share))).reshape(prompts, EXTRA, 256)
    own_states = jnp.concatenate([ssm_state.reshape(prompts, PIECE, 256), piece], axis=1)
    projected, state, high, low, gate, factor = exchange(
        hidden, proj_weight, own_states, slot_prompt, inner_raw, gate_raw, step_raw, decay_log[None, :],
        step_bias[None, :], conv_weight, conv_bias,
    )
    conv_rows = state[:, PIECE:, :].reshape(16, EXTRA * 256)[:, : 3 * share].reshape(16, 3, share)
    conv_rows = conv_rows.transpose(1, 0, 2).reshape(3, 16 * share)
    return after(
        slot_len, projected, conv_weight, conv_bias, conv_rows, state, inner_raw, factor, high, low, gate,
        norm_gain[None, :],
    )


def solution(mesh):
    rows = P(("dp", "fsdp"), None)
    in_specs = (
        rows, rows, rows, rows, P("fsdp", None), P(), P(), P(), P(), P(),
        P("dp", "fsdp", None, None), P("dp", None, None), P(("dp", "fsdp")), P(("dp", "fsdp")),
    )
    return jax.shard_map(on_device, mesh=mesh, in_specs=in_specs, out_specs=rows, check_vma=False)
```

time: 351 us -> 129 us (0.37)
  the two profiles are of different devices: /device:TPU:1 before, /device:TPU:7 now
where the time goes in v3:
time: 129 us
  Pallas kernels  124 us (96%)
  other arithmetic  1.88 us (1%)
  local copies, waits for them, and re-layouts  1.66 us (1%)
  between operations  1.55 us (1%)
    pallas_call x1, Pallas kernels, exchange(): pl.pallas_call(exchange_kernel, in_specs=[pl.BlockSpec(memory_space=pltpu...  109 us
    pallas_call x1, Pallas kernels, after(): pl.pallas_call(after_kernel, grid=(groups,), in_specs=[pl.BlockSpec(memor...  14.2 us

profile of v3, /device:TPU:7, one launch (start us, length us, event | category | flops | bytes accessed | tf_op | source)
XLA Modules:
  0.0 128.7 jit_solution(9460729621252231211)
XLA Ops:
  0.0 0.0 copy-start
  1.3 0.0 copy-done
  1.4 1.9 %pad_maximum_fusion.states_ref = bf16[2,528,256]{2,1,0:T(8,128)(2,1)} fusion(bf16[2,16,256]{2,1,0:T(8,128)(2,1)S(1)} %bitcast.25, bf16[2,512,256]{2,1,0:T(8,128)(2,1)} %bitcast.18), kind=kLoop, calls=%fused_computation | loop fusion | flops 1081344 | bytes 1081344 | tf_op jit(solution)/shard_map/concatenate | solution.py:556
  3.3 109.4 %exchange.1 = (f32[256,2048]{1,0:T(8,128)}, bf16[16,528,256]{2,1,0:T(8,128)(2,1)}, bf16[256,8192]{1,0:T(8,128)(2,1)}, bf16[256,8192]{1,0:T(8,128)(2,1)}, f32[256,8192]{1,0:T(8,128)}, /*index=5*/f32[16,8192]{1,0:T(8,128)}) custom-call(s32[1]{0:T(128)S(6)} %copy.19.prompt_ref, bf16[256,8192]{1,0:T(8,128)(2,1)} %hidden_ref.1, bf16[512,2048]{1,0:T(8,128)(2,1)} %weight_ref.1, ...), custom_call_target="tpu_custom_call" | custom-call | flops 8999999488 | bytes 33554432 | tf_op jit(solution)/shard_map/exchange/pallas_call | solution.py:501
  112.7 0.9 slice.6
  113.7 0.7 reshape.22
  114.4 14.2 %scan_and_norm.1 = bf16[256,8192]{1,0:T(8,128)(2,1)} custom-call(s32[1]{0:T(128)S(6)} %copy.20.length_ref, f32[256,2048]{1,0:T(8,128)} %get-tuple-element.11.b_ref.c_ref, f32[256,2048]{1,0:T(8,128)} %get-tuple-element.11.b_ref.c_ref, f32[4,10240]{1,0:T(4,128)} %taps_ref.3, f32[4,10240]{1,0:T(4,128)} %taps_ref.3, f32[4,10240]{1,0:T(4,128)} %taps_ref.3, ...), custom_call_target="tpu_custom_call" | custom-call | tf_op jit(solution)/shard_map/scan_and_norm/pallas_call | solution.py:93
  (5 shorter events, 0.1 us)
Async XLA Ops:
  0.0 1.3 %copy-start = (bf16[2,3,10240]{2,0,1:T(2,128)(2,1)S(1)}, bf16[2,3,10240]{2,0,1:T(2,128)(2,1)}, u32[]{:S(2)}) copy-start(bf16[2,3,10240]{2,0,1:T(2,128)(2,1)} %param.25) | copy-start | bytes 368644

commit v4 on v3

--- a/solution.py
+++ b/solution.py
@@ -40,20 +40,32 @@
 
 
 def after_kernel(
-    length_ref, b_ref, c_ref, b_taps_ref, c_taps_ref, taps_ref, b_bias_ref, c_bias_ref, bias_ref,
-    b_first_ref, c_first_ref, first_ref, state_ref, inner_ref, factor_ref,
-    high_ref, low_ref, gate_ref, gain_ref, out_ref, pad_ref, head_pad_ref, gated_ref,
+    length_ref, b_ref, c_ref, taps_ref, bias_ref, extra_ref, factor_ref, gain_ref, state_ref, inner_ref,
+    high_ref, low_ref, gate_ref, out_ref, pad_ref, head_pad_ref, gated_ref, first_ref,
 ):
-    count = b_ref.shape[0]
+    count, n = b_ref.shape
     features = high_ref.shape[1]
-
-    def channel(pad, rows, first, taps, bias):
-        return silu(convolve(pad, rows[...].astype(F32), first[...].astype(F32), taps[...], bias[...]))
-
-    head_rows = channel(head_pad_ref, inner_ref, first_ref, taps_ref, bias_ref) * factor_ref[...]
+    groups = gain_ref.shape[1] // features
+    group = pl.program_id(0)
+
+    @pl.when(group == 0)
+    def _():
+        share = first_ref.shape[1] // extra_ref.shape[0]
+        for owner in range(extra_ref.shape[0]):
+            held = extra_ref[owner].astype(F32)
+            for at, low in enumerate(range(0, share, 256)):
+                many = min(256, share - low)
+                first_ref[0:3, owner * share + low : owner * share + low + many] = held[3 * at : 3 * at + 3, :many]
+
+    def channel(pad, rows, low):
+        cols = pl.ds(pl.multiple_of(low, 128), rows.shape[1])
+        return silu(convolve(pad, rows[...].astype(F32), first_ref[0:3, cols], taps_ref[:, cols], bias_ref[:, cols]))
+
+    wide = pl.ds(pl.multiple_of(group * features, features), features)
+    head_rows = channel(head_pad_ref, inner_ref, group * features) * factor_ref[:, wide]
     head_high, head_low = split_two(head_rows)
-    b_high, b_low = split_two(channel(pad_ref, b_ref, b_first_ref, b_taps_ref, b_bias_ref))
-    c_high, c_low = split_two(channel(pad_ref, c_ref, c_first_ref, c_taps_ref, c_bias_ref))
+    b_high, b_low = split_two(channel(pad_ref, b_ref, groups * features + group * n))
+    c_high, c_low = split_two(channel(pad_ref, c_ref, groups * (features + n) + group * n))
     scores = dot_nt(c_high, b_high) + (dot_nt(c_high, b_low) + dot_nt(c_low, b_high))
     place = lax.broadcasted_iota(jnp.int32, (count, count), 0)
     other = lax.broadcasted_iota(jnp.int32, (count, count), 1)
@@ -75,33 +87,31 @@
     mean = jnp.sum(squares, axis=1, keepdims=True) * (1.0 / features)
     row = lax.broadcasted_iota(jnp.int32, (count, 1), 0)
     scale = jnp.where(row < length_ref[0], lax.rsqrt(mean + 1e-05), 0.0)
+    gain = gain_ref[:, wide]
     for low in range(0, features, PIECE):
         cols = slice(low, low + PIECE)
-        out_ref[:, cols] = (gated_ref[:, cols] * scale * gain_ref[:, cols]).astype(BF16)
+        out_ref[:, cols] = (gated_ref[:, cols] * scale * gain[:, cols]).astype(BF16)
 
 
 def after(
-    length, projected, conv_weight, conv_bias, conv_rows, state, inner_raw, factor, high, low, gate, norm_gain
+    length, projected, conv_weight, conv_bias, state, inner_raw, factor, high, low, gate, norm_gain
 ):
     count, features = high.shape
     n = state.shape[2]
     groups = projected.shape[1] // (2 * n)
     width = features // groups
-    first_b = features // n
-    at = lambda rows, base: pl.BlockSpec((rows, n), lambda g, base=base: (0, base + g))
+    at = lambda base: pl.BlockSpec((count, n), lambda g: (0, base + g))
     wide = lambda rows: pl.BlockSpec((rows, width), lambda g: (0, g))
+    whole = pl.BlockSpec(memory_space=pltpu.VMEM)
     return pl.pallas_call(
         after_kernel,
         grid=(groups,),
         in_specs=[
             pl.BlockSpec(memory_space=pltpu.SMEM),
-            at(count, 0), at(count, groups),
-            at(4, first_b), at(4, first_b + groups), wide(4),
-            at(1, first_b), at(1, first_b + groups), wide(1),
-            at(3, first_b), at(3, first_b + groups), wide(3),
+            at(0), at(groups), whole, whole,
+            pl.BlockSpec((16, EXTRA, n), lambda g: (0, PIECE // EXTRA, 0)), whole, whole,
             pl.BlockSpec((width // PIECE, PIECE, n), lambda g: (g, 0, 0)),
-            wide(HEAD_ROWS), wide(HEAD_ROWS),
-            wide(count), wide(count), wide(count), wide(1),
+            wide(HEAD_ROWS), wide(count), wide(count), wide(count),
         ],
         out_specs=wide(count),
         out_shape=jax.ShapeDtypeStruct((count, features), BF16),
@@ -109,12 +119,13 @@
             pltpu.VMEM((count + 8, n), F32),
             pltpu.VMEM((HEAD_ROWS + 8, width), F32),
             pltpu.VMEM((count, width), F32),
+            pltpu.VMEM((8, conv_weight.shape[1]), F32),
         ],
         compiler_params=pltpu.CompilerParams(vmem_limit_bytes=62 * 2**20),
         name="scan_and_norm",
     )(
-        length, projected, projected, conv_weight, conv_weight, conv_weight, conv_bias, conv_bias, conv_bias,
-        conv_rows, conv_rows, conv_rows, state, inner_raw, factor, high, low, gate, norm_gain,
+        length, projected, projected, conv_weight, conv_bias, state, factor, norm_gain, state,
+        inner_raw, high, low, gate,
     )
 
 
@@ -129,7 +140,7 @@
 
 def exchange_kernel(
     prompt_ref, hidden_ref, weight_ref, states_ref, inner_ref, gate_ref, step_ref, decay_ref,
-    step_bias_ref, taps_ref, bias_ref,
+    step_bias_ref, taps_ref, bias_ref, prompt_rows_ref,
     projected_ref, arrived_ref, high_ref, low_ref, gate_out_ref, factor_ref,
     shared, direct, rows, states_a, states_b, outgoing, prompts, prompt_words, partial, total, landed,
     partial_d, total_d, landed_d, inner, gate, gate_out, pad_ref, heads_ref, grow_ref, fall_ref,
@@ -207,7 +218,7 @@
     unit_here, unit_across = dp_at(y, z), dp_at(y + 2, z)
 
     def own_states(half, slot, to):
-        src = states_ref.at[:, pl.ds(*HALVES[half])]
+        src = states_ref.at[:, pl.ds(*HALVES[0])] if half == 0 else unit(unit_here, 1)
         send(src, unit(unit_here, half), s_send.at[half, slot], s_recv.at[half, slot], to)
 
     def own_along(half):
@@ -275,8 +286,18 @@
     send(own_shared(0), shared_at(0, x, core), w_send.at[1], w_recv.at[1], x_down)
     lax.fori_loop(0, 8, tell, 0)
     keep_states = [
-        local(states_ref.at[:, pl.ds(*HALVES[half])], unit(unit_here, half), (2, 15)[half]) for half in range(2)
+        local(states_ref.at[:, pl.ds(256 * half, 256)], unit(unit_here, half).at[:, pl.ds(0, 256)], (2, 15)[half])
+        for half in range(2)
     ]
+    share = prompt_rows_ref.shape[2] // 16
+    for which in range(2):
+        cols = pl.ds(pl.multiple_of(fsdp * share, 128), share)
+        held = [prompt_rows_ref[tap, :, cols].astype(F32)[which : which + 1] for tap in range(3)]
+        held = jnp.concatenate(held, axis=0)
+        parts = [held[:, low : min(low + 256, share)] for low in range(0, share, 256)]
+        parts[-1] = jnp.concatenate([parts[-1], jnp.zeros((3, 256 - parts[-1].shape[1]), F32)], axis=1)
+        parts.append(jnp.zeros((EXTRA - 3 * len(parts), 256), F32))
+        states_b[2 * unit_here + which, pl.ds(256, EXTRA)] = jnp.concatenate(parts, axis=0).astype(BF16)
     theirs = pl.ds(pl.multiple_of((1 - parity) * depth, depth), depth)
     ours = pl.ds(pl.multiple_of(parity * depth, depth), depth)
     keep_rows = local(hidden_ref.at[:, ours], rows.at[pl.ds(count, count)], 3)
@@ -322,6 +343,8 @@
     lax.fori_loop(0, 3, prepare, 0)
 
     across_along(0)
+    for copy in keep_states:
+        copy.wait()
     own_states(1, 0, across)
     hop(0, y, 1, 5)
     landing(shared_at(0, x + 3, core), w_recv.at[0])
@@ -376,13 +399,13 @@
 
         lax.fori_loop(0, 8, step, 0)
 
-    for copy in keep_states:
-        copy.wait()
     lax.fori_loop(0, 8, heard, 0)
     local(prompts, prompt_words, 11).wait()
     far_states(0)
     give(0)
     hop(1, y, 1, 5)
+    along_z(0)
+    along_z(1)
     landing(shared_at(0, x + 2, core, 0, 256), w_recv.at[2])
     landing(shared_at(0, x + 2, core, 256, 256), w_recv.at[3])
     to_sibling(shared_at(0, x + 2, core), 7)
@@ -396,10 +419,9 @@
     send(second, second, x_send.at[3], x_recv.at[3], x_down)
     to_sibling(direct_at(x + 1, core), 9)
     lax.fori_loop(3, 6, prepare, 0)
+    along_z(2)
     far_states(1)
     give(1)
-    for at in range(3):
-        along_z(at)
 
     def multiply(weights_of, mine_to, theirs_to, theirs_in, slot):
         theirs_to[...] = dot_nn(rows[:count, :], weights_of[...])
@@ -442,11 +464,34 @@
             leave = [local(inner, high_ref, 12), local(gate, low_ref, 13), local(gate_out, gate_out_ref, 14)]
     multiply_shared(3, (11, 12, 13))
     multiply_shared(1, (14, 15, 16))
-    for at, dx in enumerate(FAR):
-        landing(shared_at(2, x + dx, core, 0, 256), z_recv.at[6 + at])
-        landing(shared_at(2, x + dx, core, 256, 256), z_recv.at[9 + at])
-        to_sibling(shared_at(2, x + dx, core), 17 + at)
-    multiply_shared(2, (17, 18, 19))
+    def last_part(xx, start, finish):
+        deep = pl.ds(pl.multiple_of((xx % 4) * 1024, 1024), 1024)
+        piece = shared[(z + 2) % 4, deep]
+        theirs_now = dot_nn(rows[:count, deep], piece)
+        partial[2] = theirs_now if start else partial[2] + theirs_now
+        if finish:
+            send(partial.at[2], landed.at[2], t_send.at[2], t_recv.at[2], partner)
+        own_now = dot_nn(rows[count:, deep], piece)
+        total[2] = own_now if start else total[2] + own_now
+
+    def last_lands(at):
+        here = x + FAR[at]
+        landing(shared_at(2, here, core, 0, 256), z_recv.at[6 + at])
+        landing(shared_at(2, here, core, 256, 256), z_recv.at[9 + at])
+        to_sibling(shared_at(2, here, core), 17 + at)
+
+    keep[2].wait()
+    landing(shared_at(2, x, core + 1), d_recv.at[2])
+    last_part(x, True, False)
+    last_lands(0)
+    last_lands(1)
+    landing(shared_at(2, x + FAR[0], core + 1), d_recv.at[17])
+    last_part(x + FAR[0], False, False)
+    last_lands(2)
+    landing(shared_at(2, x + FAR[1], core + 1), d_recv.at[18])
+    last_part(x + FAR[1], False, False)
+    landing(shared_at(2, x + FAR[2], core + 1), d_recv.at[19])
+    last_part(x + FAR[2], False, True)
 
     landing(landed_d, t_recv.at[4])
     projected_ref[:, :DIRECT] = total_d[...] + landed_d[...]
@@ -489,7 +534,7 @@
 
 
 def exchange(
-    hidden, weight, states, prompt, inner_raw, gate_raw, step_raw, decay_log, step_bias, conv_weight, conv_bias
+    hidden, weight, states, conv_state, prompt, inner_raw, gate_raw, step_raw, decay_log, step_bias, conv_weight, conv_bias
 ):
     count, features = inner_raw.shape
     columns = weight.shape[1]
@@ -500,7 +545,7 @@
     inside = pl.BlockSpec(memory_space=pltpu.VMEM)
     return pl.pallas_call(
         exchange_kernel,
-        in_specs=[pl.BlockSpec(memory_space=pltpu.SMEM)] + [anywhere] * 5 + [inside] * 5,
+        in_specs=[pl.BlockSpec(memory_space=pltpu.SMEM)] + [anywhere] * 5 + [inside] * 6,
         out_specs=[inside, anywhere, anywhere, anywhere, anywhere, inside],
         out_shape=[
             jax.ShapeDtypeStruct((count, columns), F32),
@@ -540,7 +585,10 @@
         ),
         cost_estimate=pl.CostEstimate(flops=9 * 10**9, bytes_accessed=2**25, transcendentals=0),
         name="exchange",
-    )(prompt, hidden, weight, states, inner_raw, gate_raw, step_raw, decay_log, step_bias, conv_weight, conv_bias)
+    )(
+        prompt, hidden, weight, states, inner_raw, gate_raw, step_raw, decay_log, step_bias, conv_weight,
+        conv_bias, conv_state.transpose(1, 0, 2),
+    )
 
 
 def on_device(
@@ -548,20 +596,13 @@
     norm_gain, ssm_state, conv_state, slot_prompt, slot_len,
 ):
     conv_bias = conv_bias[None, :]
-    part = lax.axis_index("fsdp")
-    share = conv_state.shape[2] // 16
-    prompts = conv_state.shape[0]
-    piece = lax.dynamic_slice_in_dim(conv_state, part * share, share, axis=2).reshape(prompts, 3 * share)
-    piece = jnp.pad(piece, ((0, 0), (0, EXTRA * 256 - 3 * share))).reshape(prompts, EXTRA, 256)
-    own_states = jnp.concatenate([ssm_state.reshape(prompts, PIECE, 256), piece], axis=1)
+    own_states = ssm_state.reshape(ssm_state.shape[0], PIECE, ssm_state.shape[3])
     projected, state, high, low, gate, factor = exchange(
-        hidden, proj_weight, own_states, slot_prompt, inner_raw, gate_raw, step_raw, decay_log[None, :],
+        hidden, proj_weight, own_states, conv_state, slot_prompt, inner_raw, gate_raw, step_raw, decay_log[None, :],
         step_bias[None, :], conv_weight, conv_bias,
     )
-    conv_rows = state[:, PIECE:, :].reshape(16, EXTRA * 256)[:, : 3 * share].reshape(16, 3, share)
-    conv_rows = conv_rows.transpose(1, 0, 2).reshape(3, 16 * share)
     return after(
-        slot_len, projected, conv_weight, conv_bias, conv_rows, state, inner_raw, factor, high, low, gate,
+        slot_len, projected, conv_weight, conv_bias, state, inner_raw, factor, high, low, gate,
         norm_gain[None, :],
     )
 

time: 129 us -> 122 us (0.946)
  the two profiles are of different devices: /device:TPU:7 before, /device:TPU:1 now
where the time goes in v4:
time: 122 us
  Pallas kernels  121 us (99%)
  between operations  1.31 us (1%)
    pallas_call x1, Pallas kernels, exchange(): pl.pallas_call(exchange_kernel, in_specs=[pl.BlockSpec(memory_space=pltpu...  107 us
    pallas_call x1, Pallas kernels, after(): pl.pallas_call(after_kernel, grid=(groups,), in_specs=[pl.BlockSpec(memor...  14.1 us

profile of v4, /device:TPU:1, one launch (start us, length us, event | category | flops | bytes accessed | tf_op | source)
XLA Modules:
  0.0 122.3 jit_solution(17618156560658926784)
XLA Ops:
  1.3 106.8 %exchange.1 = (f32[256,2048]{1,0:T(8,128)}, bf16[16,528,256]{2,1,0:T(8,128)(2,1)}, bf16[256,8192]{1,0:T(8,128)(2,1)}, bf16[256,8192]{1,0:T(8,128)(2,1)}, f32[256,8192]{1,0:T(8,128)}, /*index=5*/f32[16,8192]{1,0:T(8,128)}) custom-call(s32[1]{0:T(128)S(6)} %copy.15.prompt_ref, bf16[256,8192]{1,0:T(8,128)(2,1)} %hidden_ref.1, bf16[512,2048]{1,0:T(8,128)(2,1)} %weight_ref.1, ...), custom_call_target="tpu_custom_call" | custom-call | flops 8999999488 | bytes 33554432 | tf_op jit(solution)/shard_map/exchange/pallas_call | solution.py:546
  108.2 14.1 %scan_and_norm.1 = bf16[256,8192]{1,0:T(8,128)(2,1)} custom-call(s32[1]{0:T(128)S(6)} %copy.16.length_ref, f32[256,2048]{1,0:T(8,128)} %get-tuple-element.11.b_ref.c_ref, f32[256,2048]{1,0:T(8,128)} %get-tuple-element.11.b_ref.c_ref, f32[4,10240]{1,0:T(4,128)} %taps_ref.3, f32[1,10240]{1,0:T(1,128)} %bitcast.7, ...), custom_call_target="tpu_custom_call" | custom-call | tf_op jit(solution)/shard_map/scan_and_norm/pallas_call | solution.py:106

commit v5 on v4

--- a/solution.py
+++ b/solution.py
@@ -357,8 +357,8 @@
     to_sibling(shared_at(0, x + 1, core), 6)
     send(own_direct, direct_at(x, core), x_send.at[0], x_recv.at[0], x_up)
     send(own_direct, direct_at(x, core), x_send.at[1], x_recv.at[1], x_down)
+    own_along(1)
     hop(0, y + 2, 3, 7)
-    own_along(1)
     across_along(1)
     send(hidden_ref.at[:, theirs], rows.at[pl.ds(0, count)], h_send.at[0], h_recv.at[0], partner)
 
@@ -372,10 +372,11 @@
         return 0
 
     def give(half):
-        def step(i, _):
+        def step(turn, _):
+            i = ((2 + 3 * (turn // 2)) % 4) * 2 + turn % 2
             to_x, to_core = (x + i // 2) % 4, (core + i % 2) % 2
             at = to_x * 2 + to_core
-            for kind in range(3):
+            for kind in (1, 2, 0):
                 low, size = SPANS[kind][half]
                 span = pl.ds(low, size)
                 outgoing[min(kind, 1), i, span] = states[half][

time: 122 us -> 122 us (level)
  no operation moved by 1% of the time
where the time goes in v5:
time: 122 us
  Pallas kernels  121 us (99%)
  between operations  1.31 us (1%)
    pallas_call x1, Pallas kernels, exchange(): pl.pallas_call(exchange_kernel, in_specs=[pl.BlockSpec(memory_space=pltpu...  107 us
    pallas_call x1, Pallas kernels, after(): pl.pallas_call(after_kernel, grid=(groups,), in_specs=[pl.BlockSpec(memor...  14.1 us

profile of v5, /device:TPU:1, one launch (start us, length us, event | category | flops | bytes accessed | tf_op | source)
XLA Modules:
  0.0 122.1 jit_solution(6027612958629275897)
XLA Ops:
  1.3 106.7 %exchange.1 = (f32[256,2048]{1,0:T(8,128)}, bf16[16,528,256]{2,1,0:T(8,128)(2,1)}, bf16[256,8192]{1,0:T(8,128)(2,1)}, bf16[256,8192]{1,0:T(8,128)(2,1)}, f32[256,8192]{1,0:T(8,128)}, /*index=5*/f32[16,8192]{1,0:T(8,128)}) custom-call(s32[1]{0:T(128)S(6)} %copy.15.prompt_ref, bf16[256,8192]{1,0:T(8,128)(2,1)} %hidden_ref.1, bf16[512,2048]{1,0:T(8,128)(2,1)} %weight_ref.1, ...), custom_call_target="tpu_custom_call" | custom-call | flops 8999999488 | bytes 33554432 | tf_op jit(solution)/shard_map/exchange/pallas_call | solution.py:547
  108.0 14.1 %scan_and_norm.1 = bf16[256,8192]{1,0:T(8,128)(2,1)} custom-call(s32[1]{0:T(128)S(6)} %copy.16.length_ref, f32[256,2048]{1,0:T(8,128)} %get-tuple-element.11.b_ref.c_ref, f32[256,2048]{1,0:T(8,128)} %get-tuple-element.11.b_ref.c_ref, f32[4,10240]{1,0:T(4,128)} %taps_ref.3, f32[1,10240]{1,0:T(1,128)} %bitcast.7, ...), custom_call_target="tpu_custom_call" | custom-call | tf_op jit(solution)/shard_map/scan_and_norm/pallas_call | solution.py:106
